TPU v7x, 512 devices: a whole 4x8x8 slice. The times are simulated.
512 devices in a mesh: wide: 64 (over z_lo, y, core), narrow: 8 (over x, z_hi).
Axes of the slice: x: 4, y: 8, z: 8 (z_hi: 2, z_lo: 4; z = z_hi * 4 + z_lo), core: 2. Of those that a mesh axis runs over, the one named last changes fastest.
Arguments:
- features: bfloat16 [16, 1024, 2, 1024], P(None, 'wide', None, 'narrow'), may hold values from -6 to 6
- cotangent: bfloat16 [16, 1024, 2, 1024], P(None, 'wide', None, 'narrow'), may hold values from -6 to 6
- coarse_weight: bfloat16 [32, 16, 3, 3, 3], replicated, may hold values from -0.3125 to 0.3125
- fine_weight: bfloat16 [16, 48, 3, 3, 3], replicated, may hold values from -0.15625 to 0.15625
Outputs:
- output: bfloat16 [16, 1024, 2, 1024], P(None, 'wide', None, 'narrow')
- grad_features: bfloat16 [16, 1024, 2, 1024], P(None, 'wide', None, 'narrow')
- grad_fine: float32 [16, 48, 3, 3, 3], replicated
- grad_coarse: float32 [32, 16, 3, 3, 3], replicated
All inputs are finite; a program needn't handle non-finite values.
Results may differ from a plain program's by a relative error of at most 0.012.
Values may be sent and summed in bfloat16 or wider, within the bound.
A program may use at most 64 MiB of HBM per device.

v0:
```python
import math

import jax
import jax.numpy as jnp
from jax import lax
from jax.sharding import PartitionSpec as P


def extended_2(array, sides, width):
    for axis, dim in sides:
        count, length = (lax.axis_size(axis), array.shape[dim])
        up = [(i, (i + 1) % count) for i in range(count - 1)]
        down = [(j, i) for i, j in up]
        last = lax.slice_in_dim(array, length - width, length, axis=dim)
        first = lax.slice_in_dim(array, 0, width, axis=dim)
        before = lax.ppermute(last, axis, up)
        after = lax.ppermute(first, axis, down)
        array = jnp.concatenate([before, array, after], axis=dim)
    return array


def shortened(array):
    return jax.tree.map(lambda a: a.astype(jnp.bfloat16) if a.dtype == jnp.float32 else a, array)


def correlate(padded, kernel):
    result = lax.conv_general_dilated(
        padded[None],
        kernel,
        (1, 1, 1),
        "VALID",
        dimension_numbers=("NCHWD", "OIHWD", "NCHWD"),
        preferred_element_type=jnp.float32,
    )
    return result[0]


def weight_grad(padded, grad):
    result = lax.conv_general_dilated(
        padded[:, None],
        grad[:, None],
        (1, 1, 1),
        "VALID",
        dimension_numbers=("NCHWD", "OIHWD", "NCHWD"),
        preferred_element_type=jnp.float32,
    )
    return jnp.transpose(result, (1, 0, 2, 3, 4))


def flipped(kernel):
    return jnp.transpose(kernel[:, :, ::-1, ::-1, ::-1], (1, 0, 2, 3, 4))


def pool_sum(field):
    chans, rows, planes, cols = field.shape
    return field.reshape(chans, rows // 2, 2, planes // 2, 2, cols // 2, 2).sum(axis=(2, 4, 6))


def upsample(field):
    chans, rows, planes, cols = field.shape
    spread = jnp.broadcast_to(
        field[:, :, None, :, None, :, None], (chans, rows, 2, planes, 2, cols, 2)
    )
    return spread.reshape(chans, 2 * rows, 2 * planes, 2 * cols)


def silu_slope(value):
    sig = jax.nn.sigmoid(value)
    return sig * (1.0 + value * (1.0 - sig))


def fine_padded(field):
    extended = extended_2(field, (("wide", 1), ("narrow", 3)), 1)
    return jnp.pad(extended, ((0, 0), (0, 0), (1, 1), (0, 0)))


def coarse_padded(field):
    extended = extended_2(field, ((("wide", "narrow"), 1),), 1)
    return jnp.pad(extended, ((0, 0), (0, 0), (1, 1), (1, 1)))


def into_coarse(field):
    return jax.tree.map(
        lambda part, own: part.astype(own.dtype),
        lax.all_to_all(shortened(field), "narrow", split_axis=1, concat_axis=3, tiled=True),
        field,
    )


def into_fine(field):
    return jax.tree.map(
        lambda part, own: part.astype(own.dtype),
        lax.all_to_all(shortened(field), "narrow", split_axis=3, concat_axis=1, tiled=True),
        field,
    )


def shards(features, cotangent, coarse_weight, fine_weight):
    channels = features.shape[0]
    pooled = (pool_sum(features.astype(jnp.float32)) / 8.0).astype(jnp.bfloat16)
    coarse_ext = coarse_padded(into_coarse(pooled))
    coarse_pre = correlate(coarse_ext, coarse_weight)
    coarse_act = jax.nn.silu(coarse_pre).astype(jnp.bfloat16)
    upsampled = upsample(into_fine(coarse_act))
    joined_ext = fine_padded(jnp.concatenate([features, upsampled], 0))
    cotangent_ext = fine_padded(cotangent)
    output = correlate(joined_ext, fine_weight).astype(jnp.bfloat16)
    local_fine = weight_grad(joined_ext, cotangent)
    grad_joined = correlate(cotangent_ext, flipped(fine_weight))
    grad_act = into_coarse(pool_sum(grad_joined[channels:]).astype(jnp.bfloat16))
    grad_pre = (grad_act.astype(jnp.float32) * silu_slope(coarse_pre)).astype(jnp.bfloat16)
    local_coarse = weight_grad(coarse_ext, grad_pre)
    grad_pooled = correlate(coarse_padded(grad_pre), flipped(coarse_weight)).astype(jnp.bfloat16)
    grad_features = (
        grad_joined[:channels] + upsample(into_fine(grad_pooled)).astype(jnp.float32) / 8.0
    ).astype(jnp.bfloat16)
    fine_total, coarse_total = lax.psum((local_fine, local_coarse), ("wide", "narrow"))
    all_cells = (
        features.shape[1]
        * features.shape[2]
        * features.shape[3]
        * lax.axis_size("wide")
        * lax.axis_size("narrow")
    )
    return (
        output,
        grad_features,
        fine_total / math.sqrt(all_cells),
        coarse_total / math.sqrt(all_cells // 8),
    )


def solution(mesh):
    placed = (P(None, "wide", None, "narrow"), P(None, "wide", None, "narrow"), P(), P())
    return jax.shard_map(
        shards,
        mesh=mesh,
        in_specs=placed,
        out_specs=(P(None, "wide", None, "narrow"), P(None, "wide", None, "narrow"), P(), P()),
        check_vma=False,
    )
```

profile of v0, /device:TPU:1, one launch (start us, length us, event | category | flops | bytes accessed | tf_op | source)
XLA Modules:
  0.0 639.0 jit_solution(16950988302908629010)
XLA Ops:
  8.0 4.6 collective-permute-start.6
  12.6 5.5 collective-permute-start.7
  18.1 1.3 convert_reduce_fusion
  21.0 1.3 collective-permute-start.9
  22.3 8.1 %collective-permute-start.8 = (bf16[16,18,2,1]{3,2,1,0:T(2,128)(2,1)S(1)}, bf16[16,18,2,1]{3,2,1,0:T(2,128)(2,1)S(1)}, u32[]{:S(2)}, u32[]{:S(2)}) collective-permute-start(bf16[16,18,2,1]{3,2,1,0:T(2,128)(2,1)S(1)} %get-tuple-element.36), channel_id=1, source_target_pairs={{0,1},{1,2},{2,3},{3,4},{4,5},{5,6},{6,7},{8,9},{9,10},{10,11},{11... | collective-permute-start | bytes 3464 | tf_op jit(solution)/shard_map/ppermute | solution.py:16
  31.3 10.0 %all-to-all-start = ((bf16[8,2,512]{2,1,0:T(2,128)(2,1)}), bf16[8,2,512]{2,1,0:T(2,128)(2,1)S(1)}, u32[]{:S(2)}, u32[]{:S(2)}) async-start(bf16[8,2,512]{2,1,0:T(2,128)(2,1)} %reshape.289), calls=%async_computation | async-start | bytes 32768 | tf_op jit(solution)/shard_map/all_to_all | solution.py:85
  41.3 3.8 copy.231
  45.1 1.3 fusion.54
  46.7 1.8 reshape.286
  48.5 5.1 copy.219
  53.6 1.0 slice.64
  54.7 5.0 fusion.26
  60.4 2.0 copy.221
  62.6 8.5 %collective-permute-start.1 = (bf16[16,1,1,512]{3,0,2,1:T(8,128)(2,1)S(1)}, bf16[16,1,1,512]{3,0,2,1:T(8,128)(2,1)S(1)}, u32[]{:S(2)}, u32[]{:S(2)}) collective-permute-start(bf16[16,1,1,512]{3,0,2,1:T(8,128)(2,1)S(1)} %all_to_all.11), channel_id=1, source_target_pairs={{1,0},{2,1},{3,2},{4,3},{5,4},{6,5},{7,6},{8,7},{9,8},{10,9},{11,1... | collective-permute-start | bytes 49160 | tf_op jit(solution)/shard_map/ppermute | solution.py:17
  71.1 2.1 collective-permute-start
  73.2 1.9 slice_reduce_fusion
  75.1 1.8 reduce_sum.37
  78.6 10.8 %all-to-all-start.2 = ((bf16[8,2,1024]{2,1,0:T(2,128)(2,1)}), bf16[8,2,1024]{2,1,0:T(2,128)(2,1)S(1)}, u32[]{:S(2)}, u32[]{:S(2)}) async-start(bf16[8,2,1024]{2,1,0:T(2,128)(2,1)} %reshape.287), calls=%async_computation.2 | async-start | bytes 65536 | tf_op jit(solution)/shard_map/all_to_all | solution.py:85
  89.4 2.8 copy.220
  92.2 2.8 reshape.252
  97.0 1.2 fusion.46
  99.3 2.0 copy.233
  101.6 8.2 %collective-permute-start.11 = (bf16[32,1,1,512]{3,0,2,1:T(8,128)(2,1)S(1)}, bf16[32,1,1,512]{3,0,2,1:T(8,128)(2,1)S(1)}, u32[]{:S(2)}, u32[]{:S(2)}) collective-permute-start(bf16[32,1,1,512]{3,0,2,1:T(8,128)(2,1)S(1)} %get-tuple-element.40), channel_id=1, source_target_pairs={{1,0},{2,1},{3,2},{4,3},{5,4},{6,5},{7,6},{8,7},{9,8},{10,9},{11,1... | collective-permute-start | bytes 98312 | tf_op jit(solution)/shard_map/ppermute | solution.py:17
  109.7 1.9 collective-permute-start.10
  112.4 1.5 reduce.8
  114.7 11.2 %all-to-all-start.1 = ((bf16[8,2,1024]{2,1,0:T(2,128)(2,1)}), bf16[8,2,1024]{2,1,0:T(2,128)(2,1)S(1)}, u32[]{:S(2)}, u32[]{:S(2)}) async-start(bf16[8,2,1024]{2,1,0:T(2,128)(2,1)} %reshape.291), calls=%async_computation.1 | async-start | bytes 65536 | tf_op jit(solution)/shard_map/all_to_all | solution.py:93
  126.1 5.7 fusion.101
  131.8 105.8 %psum.15 = f32[32,16,3,3,3]{0,1,4,3,2:T(8,128)S(1)} all-reduce(f32[32,16,3,3,3]{0,1,4,3,2:T(8,128)S(1)} %fusion.101), channel_id=1, replica_groups=mesh['wide'=64,'narrow'=8] {'wide','narrow'}, use_global_device_ids=true, to_apply=%region_5.6 | all-reduce | flops 13824 | bytes 110592 | tf_op jit(solution)/shard_map/psum | solution.py:117
  239.0 1.7 copy.225
  240.8 1.1 fusion.33
  242.3 1.5 reduce.9
  244.6 3.3 all-to-all-start.3
  248.9 2.9 collective-permute-start.3
  251.8 2.6 collective-permute-start.2
  254.4 2.4 all-to-all-done.3
  258.3 1.3 collective-permute-start.5
  259.6 8.3 %collective-permute-start.4 = (bf16[48,18,2,1]{3,0,2,1:T(8,128)(2,1)S(1)}, bf16[48,18,2,1]{3,0,2,1:T(8,128)(2,1)S(1)}, u32[]{:S(2)}, u32[]{:S(2)}) collective-permute-start(bf16[48,18,2,1]{3,0,2,1:T(8,128)(2,1)S(1)} %get-tuple-element.32), channel_id=1, source_target_pairs={{0,1},{1,2},{2,3},{3,4},{4,5},{5,6},{6,7},{8,9},{9,10},{10,11},{11... | collective-permute-start | bytes 10376 | tf_op jit(solution)/shard_map/ppermute | solution.py:16
  268.7 5.5 collective-permute-done.5
  275.9 2.0 fusion.111
  277.9 4.9 copy.240
  282.8 1.3 pad.22.clone
  284.5 6.5 %fusion.9 = bf16[16,2,8,17,16]{4,2,3,1,0:T(8,128)(2,1)} fusion(bf16[16,48,3,3,3]{1,0,4,3,2:T(8,128)(2,1)S(1)} %copy-done, bf16[48,18,4,1,7,2]{0,4,5,2,1,3:T(8,128)(2,1)S(1)} %slice.60, bf16[48,18,4,1,8,17]{0,4,5,2,1,3:T(8,128)(2,1)S(1)} %copy.213), kind=kOutput, calls=%fused_computation.12 | convolution fusion | flops 183638016 | bytes 1217536 | tf_op jit(solution)/shard_map/conv_general_dilated | solution.py:27
  291.0 2.7 copy.214
  295.1 1.1 fusion.110
  296.2 8.8 %copy.230 = bf16[48,1,18,4,130]{0,1,4,3,2:T(2,128)(2,1)} copy(bf16[48,1,18,4,130]{4,0,3,2,1:T(8,128)(2,1)S(1)} %fusion.110) | data formatting | bytes 1797120 | tf_op jit(solution)/shard_map/broadcast_in_dim | solution.py:40
  305.0 31.3 %fusion.100 = f32[16,48,3,3,3]{1,0,4,3,2:T(8,128)} fusion(bf16[48,1,18,4,130]{0,1,4,3,2:T(2,128)(2,1)} %copy.230, bf16[16,1,16,2,128]{0,1,4,3,2:T(2,128)(2,1)} %copy.231), kind=kOutput, calls=%fused_computation.139 | convolution fusion | flops 169869312 | bytes 1112576 | tf_op jit(solution)/shard_map/transpose | solution.py:47
  337.1 293.2 %all-reduce.6.cloned.1.call-done = f32[16,48,3,3,3]{1,0,4,3,2:T(8,128)} async-done(((f32[16,48,3,3,3]{1,0,4,3,2:T(8,128)}), f32[16,48,3,3,3]{1,0,4,3,2:T(8,128)}) %all-reduce.6.cloned.1.call-update) | async-done | bytes 82960 | tf_op jit(solution)/shard_map/psum | solution.py:117
  630.3 1.6 broadcast_multiply_fusion.1
  (107 shorter events, 21.2 us)
Async XLA Ops:
  7.2 47.5 %copy-start = (bf16[16,48,3,3,3]{1,0,4,3,2:T(8,128)(2,1)S(1)}, bf16[16,48,3,3,3]{1,0,4,3,2:T(8,128)(2,1)}, u32[]{:S(2)}) copy-start(bf16[16,48,3,3,3]{1,0,4,3,2:T(8,128)(2,1)} %param.7) | copy-start | bytes 124420
  7.2 13.4 %copy-start.4 = (bf16[16,16,2,128]{3,2,1,0:T(2,128)(2,1)S(1)}, bf16[16,16,2,128]{3,2,1,0:T(2,128)(2,1)}, u32[]{:S(2)}) copy-start(bf16[16,16,2,128]{3,2,1,0:T(2,128)(2,1)} %param.5) | copy-start | bytes 393220
  7.2 34.1 %copy-start.5 = (bf16[16,16,2,128]{3,2,1,0:T(2,128)(2,1)S(1)}, bf16[16,16,2,128]{3,2,1,0:T(2,128)(2,1)}, u32[]{:S(2)}) copy-start(bf16[16,16,2,128]{3,2,1,0:T(2,128)(2,1)} %param.4) | copy-start | bytes 393220
  8.0 12.6 %collective-permute-start.6 = (bf16[16,1,2,128]{3,2,1,0:T(2,128)(2,1)S(1)}, bf16[16,1,2,128]{3,2,1,0:T(2,128)(2,1)S(1)}, u32[]{:S(2)}, u32[]{:S(2)}) collective-permute-start(bf16[16,1,2,128]{3,2,1,0:T(2,128)(2,1)S(1)} %get-tuple-element.39), channel_id=1, source_target_pairs={{0,8},{8,16},{16,24},{24,32},{32,40},{40,48},{48,56},{56,64},{64,7... | collective-permute-start | bytes 24584 | tf_op jit(solution)/shard_map/ppermute | solution.py:16
  12.6 8.1 %collective-permute-start.7 = (bf16[16,1,2,128]{3,2,1,0:T(2,128)(2,1)S(1)}, bf16[16,1,2,128]{3,2,1,0:T(2,128)(2,1)S(1)}, u32[]{:S(2)}, u32[]{:S(2)}) collective-permute-start(bf16[16,1,2,128]{3,2,1,0:T(2,128)(2,1)S(1)} %get-tuple-element.38), channel_id=1, source_target_pairs={{8,0},{16,8},{24,16},{32,24},{40,32},{48,40},{56,48},{64,56},{72,6... | collective-permute-start | bytes 24584 | tf_op jit(solution)/shard_map/ppermute | solution.py:17
  21.0 24.1 %collective-permute-start.9 = (bf16[16,18,2,1]{3,2,1,0:T(2,128)(2,1)S(1)}, bf16[16,18,2,1]{3,2,1,0:T(2,128)(2,1)S(1)}, u32[]{:S(2)}, u32[]{:S(2)}) collective-permute-start(bf16[16,18,2,1]{3,2,1,0:T(2,128)(2,1)S(1)} %get-tuple-element.37), channel_id=1, source_target_pairs={{1,0},{2,1},{3,2},{4,3},{5,4},{6,5},{7,6},{9,8},{10,9},{11,10},{12... | collective-permute-start | bytes 3464 | tf_op jit(solution)/shard_map/ppermute | solution.py:17
  22.3 22.8 %collective-permute-start.8 = (bf16[16,18,2,1]{3,2,1,0:T(2,128)(2,1)S(1)}, bf16[16,18,2,1]{3,2,1,0:T(2,128)(2,1)S(1)}, u32[]{:S(2)}, u32[]{:S(2)}) collective-permute-start(bf16[16,18,2,1]{3,2,1,0:T(2,128)(2,1)S(1)} %get-tuple-element.36), channel_id=1, source_target_pairs={{0,1},{1,2},{2,3},{3,4},{4,5},{5,6},{6,7},{8,9},{9,10},{10,11},{11... | collective-permute-start | bytes 3464 | tf_op jit(solution)/shard_map/ppermute | solution.py:16
  31.3 31.1 %all-to-all-start = ((bf16[8,2,512]{2,1,0:T(2,128)(2,1)}), bf16[8,2,512]{2,1,0:T(2,128)(2,1)S(1)}, u32[]{:S(2)}, u32[]{:S(2)}) async-start(bf16[8,2,512]{2,1,0:T(2,128)(2,1)} %reshape.289), calls=%async_computation | async-start | bytes 32768 | tf_op jit(solution)/shard_map/all_to_all | solution.py:85
  48.5 6.2 copy-start.10
  62.6 32.4 %collective-permute-start.1 = (bf16[16,1,1,512]{3,0,2,1:T(8,128)(2,1)S(1)}, bf16[16,1,1,512]{3,0,2,1:T(8,128)(2,1)S(1)}, u32[]{:S(2)}, u32[]{:S(2)}) collective-permute-start(bf16[16,1,1,512]{3,0,2,1:T(8,128)(2,1)S(1)} %all_to_all.11), channel_id=1, source_target_pairs={{1,0},{2,1},{3,2},{4,3},{5,4},{6,5},{7,6},{8,7},{9,8},{10,9},{11,1... | collective-permute-start | bytes 49160 | tf_op jit(solution)/shard_map/ppermute | solution.py:17
  71.1 23.9 %collective-permute-start = (bf16[16,1,1,512]{3,0,2,1:T(8,128)(2,1)S(1)}, bf16[16,1,1,512]{3,0,2,1:T(8,128)(2,1)}, u32[]{:S(2)}, u32[]{:S(2)}) collective-permute-start(bf16[16,1,1,512]{3,0,2,1:T(8,128)(2,1)S(1)} %all_to_all.11), channel_id=1, source_target_pairs={{0,1},{1,2},{2,3},{3,4},{4,5},{5,6},{6,7},{7,8},{8,9},{9,10},{10,1... | collective-permute-start | bytes 49160 | tf_op jit(solution)/shard_map/ppermute | solution.py:16
  78.6 22.7 %all-to-all-start.2 = ((bf16[8,2,1024]{2,1,0:T(2,128)(2,1)}), bf16[8,2,1024]{2,1,0:T(2,128)(2,1)S(1)}, u32[]{:S(2)}, u32[]{:S(2)}) async-start(bf16[8,2,1024]{2,1,0:T(2,128)(2,1)} %reshape.287), calls=%async_computation.2 | async-start | bytes 65536 | tf_op jit(solution)/shard_map/all_to_all | solution.py:85
  92.2 4.7 copy-start.8
  92.2 4.7 copy-start.9
  101.6 136.7 %collective-permute-start.11 = (bf16[32,1,1,512]{3,0,2,1:T(8,128)(2,1)S(1)}, bf16[32,1,1,512]{3,0,2,1:T(8,128)(2,1)S(1)}, u32[]{:S(2)}, u32[]{:S(2)}) collective-permute-start(bf16[32,1,1,512]{3,0,2,1:T(8,128)(2,1)S(1)} %get-tuple-element.40), channel_id=1, source_target_pairs={{1,0},{2,1},{3,2},{4,3},{5,4},{6,5},{7,6},{8,7},{9,8},{10,9},{11,1... | collective-permute-start | bytes 98312 | tf_op jit(solution)/shard_map/ppermute | solution.py:17
  109.7 128.6 %collective-permute-start.10 = (bf16[32,1,1,512]{3,0,2,1:T(8,128)(2,1)S(1)}, bf16[32,1,1,512]{3,0,2,1:T(8,128)(2,1)S(1)}, u32[]{:S(2)}, u32[]{:S(2)}) collective-permute-start(bf16[32,1,1,512]{3,0,2,1:T(8,128)(2,1)S(1)} %get-tuple-element.40), channel_id=1, source_target_pairs={{0,1},{1,2},{2,3},{3,4},{4,5},{5,6},{6,7},{7,8},{8,9},{9,10},{10,1... | collective-permute-start | bytes 98312 | tf_op jit(solution)/shard_map/ppermute | solution.py:16
  114.7 129.9 %all-to-all-start.1 = ((bf16[8,2,1024]{2,1,0:T(2,128)(2,1)}), bf16[8,2,1024]{2,1,0:T(2,128)(2,1)S(1)}, u32[]{:S(2)}, u32[]{:S(2)}) async-start(bf16[8,2,1024]{2,1,0:T(2,128)(2,1)} %reshape.291), calls=%async_computation.1 | async-start | bytes 65536 | tf_op jit(solution)/shard_map/all_to_all | solution.py:93
  240.7 1.3 copy-start.7
  244.6 12.2 %all-to-all-start.3 = ((bf16[8,2,512]{2,1,0:T(2,128)(2,1)}), bf16[8,2,512]{2,1,0:T(2,128)(2,1)S(1)}, u32[]{:S(2)}, u32[]{:S(2)}) async-start(bf16[8,2,512]{2,1,0:T(2,128)(2,1)} %reshape.293), calls=%async_computation.3 | async-start | bytes 32768 | tf_op jit(solution)/shard_map/all_to_all | solution.py:93
  247.9 382.4 %all-reduce.6.cloned.1.call-start = ((), (), s32[]{:S(2)}) async-start(), calls=%async_computation.4 | async-start | bytes 442368 | tf_op jit(solution)/shard_map/psum | solution.py:117
  248.9 9.2 %collective-permute-start.3 = (bf16[48,1,2,128]{3,0,2,1:T(8,128)(2,1)S(1)}, bf16[48,1,2,128]{3,0,2,1:T(8,128)(2,1)S(1)}, u32[]{:S(2)}, u32[]{:S(2)}) collective-permute-start(bf16[48,1,2,128]{3,0,2,1:T(8,128)(2,1)S(1)} %get-tuple-element.35), channel_id=1, source_target_pairs={{8,0},{16,8},{24,16},{32,24},{40,32},{48,40},{56,48},{64,56},{72,6... | collective-permute-start | bytes 73736 | tf_op jit(solution)/shard_map/ppermute | solution.py:17
  251.8 6.3 collective-permute-start.2
  257.3 10.6 %copy-start.3 = (f32[16,2,1,136,16]{3,4,1,0,2:T(8,128)S(1)}, f32[16,2,1,136,16]{3,4,1,0,2:T(8,128)}, u32[]{:S(2)}) copy-start(f32[16,2,1,136,16]{3,4,1,0,2:T(8,128)} %reshape.252) | copy-start | bytes 835588
  258.3 15.9 %collective-permute-start.5 = (bf16[48,18,2,1]{3,0,2,1:T(8,128)(2,1)S(1)}, bf16[48,18,2,1]{3,0,2,1:T(8,128)(2,1)S(1)}, u32[]{:S(2)}, u32[]{:S(2)}) collective-permute-start(bf16[48,18,2,1]{3,0,2,1:T(8,128)(2,1)S(1)} %get-tuple-element.33), channel_id=1, source_target_pairs={{1,0},{2,1},{3,2},{4,3},{5,4},{6,5},{7,6},{9,8},{10,9},{11,10},{12... | collective-permute-start | bytes 10376 | tf_op jit(solution)/shard_map/ppermute | solution.py:17
  259.6 15.6 %collective-permute-start.4 = (bf16[48,18,2,1]{3,0,2,1:T(8,128)(2,1)S(1)}, bf16[48,18,2,1]{3,0,2,1:T(8,128)(2,1)S(1)}, u32[]{:S(2)}, u32[]{:S(2)}) collective-permute-start(bf16[48,18,2,1]{3,0,2,1:T(8,128)(2,1)S(1)} %get-tuple-element.32), channel_id=1, source_target_pairs={{0,1},{1,2},{2,3},{3,4},{4,5},{5,6},{6,7},{8,9},{9,10},{10,11},{11... | collective-permute-start | bytes 10376 | tf_op jit(solution)/shard_map/ppermute | solution.py:16
  275.2 0.8 copy-start.1
  284.5 9.3 %copy-start.6 = (pred[8,17]{1,0:T(8,128)(4,1)S(1)}, pred[8,17]{1,0:T(8,128)(4,1)}, u32[]{:S(2)}) copy-start(pred[8,17]{1,0:T(8,128)(4,1)} %constant.46) | copy-start | bytes 412
  293.8 1.3 copy-start.2
Sparse Core Ops, SparseCore 0:
  336.4 293.8 all-reduce.5
where the time goes:
time: 648 us; the launch traced here: 639 us
  waiting for transfers between devices  302 us (47%)
  blocking collectives  106 us (16%)
  starting transfers between devices  90.7 us (14%)
  local copies, waits for them, and re-layouts  56.7 us (9%)
  matrix products  50.9 us (8%)
  other arithmetic  18 us (3%)
  between operations  14.9 us (2%)
    psum x1, waiting for transfers between devices, shards(): lax.psum((local_fine, local_coarse), ('wide', 'narrow'))  293 us
    psum x1, blocking collectives, shards(): lax.psum((local_fine, local_coarse), ('wide', 'narrow'))  106 us
    transpose x2, matrix products, weight_grad(): return jnp.transpose(result, (1, 0, 2, 3, 4))  37 us
    ppermute x6, starting transfers between devices, extended_2(): before = lax.ppermute(last, axis, up)  27.7 us
    ppermute x6, starting transfers between devices, extended_2(): after = lax.ppermute(first, axis, down)  27.6 us
    conv_general_dilated x19, local copies, waits for them, and re-layouts, correlate(): lax.conv_general_dilated(padded[None], kernel, (1, 1, 1), 'VALID', dimens...  23.1 us
    all_to_all x2, starting transfers between devices, into_coarse(): lax.all_to_all(shortened(field), 'narrow', split_axis=1, concat_axis=3, t...  20.8 us
    all_to_all x2, starting transfers between devices, into_fine(): lax.all_to_all(shortened(field), 'narrow', split_axis=3, concat_axis=1, t...  14.5 us
  transfers between devices with their start and end apart: 17, of which 4 were waited for; matrix products, arithmetic and copies ran while one was open for 10% of the time, Pallas kernels for 0%

commit v1 on v0

v1 whole, which is shorter than its diff:
```python
import functools
import math

import jax
import jax.numpy as jnp
from jax import lax
from jax.experimental import pallas as pl
from jax.experimental.pallas import tpu as pltpu
from jax.sharding import PartitionSpec as P

F32, BF16 = jnp.float32, jnp.bfloat16
MESH = pl.DeviceIdType.MESH
VMEM = pltpu.VMEM
OUTER = 4
ROWS = 192


def dot(a, b):
    return lax.dot_general(a, b, (((1,), (0,)), ((), ())), preferred_element_type=F32)


def dot_nt(a, b):
    return lax.dot_general(a, b, (((1,), (1,)), ((), ())), preferred_element_type=F32)


def iota(shape, axis):
    return lax.broadcasted_iota(jnp.int32, shape, axis)


def halo_kernel(n_wide, n_narrow, f_ref, c_ref, ext_ref, left_ref, right_ref,
                wide32, go_left, go_right, send, recv):
    me_y, me_x = lax.axis_index("wide"), lax.axis_index("narrow")
    up, down = lax.rem(me_y + n_wide - 1, n_wide), lax.rem(me_y + 1, n_wide)
    west, east = lax.rem(me_x + n_narrow - 1, n_narrow), lax.rem(me_x + 1, n_narrow)
    near = [(up, me_x), (down, me_x), (me_y, west), (me_y, east),
            (up, west), (up, east), (down, west), (down, east)]
    barrier = pltpu.get_barrier_semaphore()
    for device in near:
        pl.semaphore_signal(barrier, inc=1, device_id=device, device_id_type=MESH)
    for k, ref in enumerate((f_ref, c_ref)):
        wide32[k] = ref[...].astype(F32)
        for j in range(32):
            part = wide32[k, pl.ds(j, 16, stride=32), :]
            ext_ref[k, 128 + 16 * j:144 + 16 * j, :] = part.astype(BF16)
    row, col = iota((16, 128), 0), iota((16, 128), 1)
    for start, buf in ((0, go_left), (124, go_right)):
        total = jnp.zeros((16, 512), F32)
        for k in range(2):
            pick = (row >= 4 * k) & (row < 4 * k + 4) & (col == start + row - 4 * k)
            total += dot_nt(pick.astype(F32).astype(BF16), ext_ref[k, 128:640, :])
        buf[...] = total.astype(BF16)
    pl.semaphore_wait(barrier, 8)
    plan = [
        (ext_ref.at[:, pl.ds(128, 128), :], ext_ref.at[:, pl.ds(640, 128), :]),
        (ext_ref.at[:, pl.ds(512, 128), :], ext_ref.at[:, pl.ds(0, 128), :]),
        (go_left, right_ref.at[:, pl.ds(128, 512)]),
        (go_right, left_ref.at[:, pl.ds(128, 512)]),
        (go_left.at[:, pl.ds(0, 128)], right_ref.at[:, pl.ds(640, 128)]),
        (go_right.at[:, pl.ds(0, 128)], left_ref.at[:, pl.ds(640, 128)]),
        (go_left.at[:, pl.ds(384, 128)], right_ref.at[:, pl.ds(0, 128)]),
        (go_right.at[:, pl.ds(384, 128)], left_ref.at[:, pl.ds(0, 128)]),
    ]
    copies = []
    for j, (src, dst) in enumerate(plan):
        copies.append(pltpu.make_async_remote_copy(
            src_ref=src, dst_ref=dst, send_sem=send.at[j], recv_sem=recv.at[j],
            device_id=near[j], device_id_type=MESH))
        copies[-1].start()
    for copy in copies:
        copy.wait()


def prepare_weights(fw_ref, cw_ref, wide_w, stack, w_fwd, w_bwd, stack_c, w_pre, w_gp):
    lane = iota((16, 128), 1)
    wide_w[...] = jnp.zeros_like(wide_w)
    wide_w[0:432, 0:48] = fw_ref[...].astype(F32)
    wide_w[432:864, 0:32] = cw_ref[...].astype(F32)

    def tap(ky, kz, kx):
        at = ((ky * 3 + kz) * 3 + kx) * 16
        return wide_w[at:at + 16, :]

    zero16 = jnp.zeros((16, 128), BF16)
    for z in range(2):
        for ky in range(3):
            base = jnp.zeros((16, 128), F32)
            for kx in range(3):
                for zz in range(2):
                    at = 32 * kx + 16 * zz
                    moved = tap(ky, zz - z + 1, kx)
                    if at:
                        moved = pltpu.roll(moved, at, 1)
                    base = jnp.where((lane >= at) & (lane < at + 16), moved, base)
            for px in range(2):
                block = (pltpu.roll(base, 32, 1) if px else base).astype(BF16)
                for py in range(2):
                    rows = (py * 2 + px) * 32 + z * 16
                    w_fwd[rows:rows + 16, (ky + py) * 128:(ky + py + 1) * 128] = block
    for py in range(2):
        idle = 3 if py == 0 else 0
        for blocks in range(4):
            rows = py * 64 + blocks * 16
            w_fwd[rows:rows + 16, idle * 128:(idle + 1) * 128] = zero16
    spans = {(0, 0): (0,), (0, 1): (1, 2), (0, 2): (), (1, 0): (), (1, 1): (0, 1), (1, 2): (2,)}
    for z in range(2):
        pair = [[tap(ky, 1 - z, kx) + tap(ky, 2 - z, kx) for kx in range(3)] for ky in range(3)]
        for py in range(2):
            for dy in range(3):
                kys = spans[py, dy]
                for px in range(2):
                    rows = (py * 2 + px) * 32 + z * 16
                    block = jnp.zeros((16, 128), F32)
                    for dx in range(3):
                        terms = [pair[ky][kx] for ky in kys for kx in spans[px, dx]]
                        if not terms:
                            continue
                        moved = pltpu.roll(functools.reduce(jnp.add, terms), (32 * dx - 16) % 128, 1)
                        block = jnp.where((lane >= 32 * dx) & (lane < 32 * dx + 32), moved, block)
                    w_fwd[rows:rows + 16, 512 + dy * 128:512 + (dy + 1) * 128] = block.astype(BF16)
    for z in range(2):
        for ky in range(3):
            for wx in range(4):
                for zz in range(2):
                    at = (z * 3 + ky) * 128 + wx * 32 + zz * 16
                    if wx == 3:
                        stack[at:at + 16, :] = zero16
                    else:
                        stack[at:at + 16, :] = tap(2 - ky, 1 + z - zz, 2 - wx).astype(BF16)
    eye = (iota((48, 128), 0) == iota((48, 128), 1)).astype(F32).astype(BF16)
    turned = dot_nt(eye, stack[...])
    w_bwd[...] = jnp.zeros_like(w_bwd)
    act = [jnp.zeros((32, 128), F32) for _ in range(4)]
    for z in range(2):
        for ky in range(3):
            at = (z * 3 + ky) * 128
            base = turned[:, at:at + 128]
            for px in range(2):
                moved = pltpu.roll(base, 32, 1) if px else base
                for py in range(2):
                    rows = (py * 2 + px) * 32 + z * 16
                    w_bwd[rows:rows + 16, (ky + py) * 128:(ky + py + 1) * 128] = moved[0:16].astype(BF16)
                    act[ky + py] = act[ky + py] + moved[16:48]
    for wy in range(4):
        w_bwd[128:160, wy * 128:(wy + 1) * 128] = act[wy].astype(BF16)
    for dy in range(3):
        block = jnp.zeros((16, 128), F32)
        for dx in range(3):
            at = 432 + ((dy * 3 + 1) * 3 + dx) * 16
            stack_c[(dy * 3 + dx) * 16:(dy * 3 + dx + 1) * 16, :] = wide_w[at:at + 16, :].astype(BF16)
            at = 432 + (((2 - dy) * 3 + 1) * 3 + 2 - dx) * 16
            moved = wide_w[at:at + 16, :]
            if dx:
                moved = pltpu.roll(moved, 32 * dx, 1)
            block = jnp.where((lane >= 32 * dx) & (lane < 32 * dx + 32), moved, block)
        w_gp[:, dy * 128:(dy + 1) * 128] = block.astype(BF16)
    w_pre[...] = dot_nt(eye[0:32], stack_c[...]).astype(BF16)


def level_kernel(n_wide, n_narrow, ext_ref, left_ref, right_ref, fw_ref, cw_ref,
                 out_ref, gf_ref, sums_ref,
                 wide_w, stack, w_fwd, w_bwd, stack_c, w_pre, w_gp,
                 fine, cot, pool, act, gpre, keep_gj, flat, turn, sums):
    me_y, me_x = lax.axis_index("wide"), lax.axis_index("narrow")
    prepare_weights(fw_ref, cw_ref, wide_w, stack, w_fwd, w_bwd, stack_c, w_pre, w_gp)
    top, bottom = me_y > 0, me_y < n_wide - 1
    first, last = me_x > 0, me_x < n_narrow - 1

    want = iota((128, 512), 1)
    want = 2 * ((want & 127) - 2) - 1 + (want >> 7)
    spread = (iota((128, 512), 0) == want).astype(F32).astype(BF16)
    side_want = iota((32, 512), 1)
    side_want = 2 * ((side_want & 127) - 2) - 1 + (side_want >> 7)
    side_row = iota((32, 512), 0)
    sides = jnp.concatenate([left_ref[...].astype(F32), right_ref[...].astype(F32)], axis=0)
    turned = jnp.transpose(sides).astype(BF16)
    for k, field in enumerate((fine, cot)):
        west = (side_row >= 4 * k) & (side_row < 4 * k + 4) & (side_want == side_row - 4 * k - 4) & first
        east = (side_row >= 16 + 4 * k) & (side_row < 20 + 4 * k) & (side_want == side_row - 16 - 4 * k + 128) & last
        spread_side = (west | east).astype(F32).astype(BF16)
        for part in range(6):
            at = part * 128
            got = dot(ext_ref[k, at:at + 128, :], spread) + dot(turned[at:at + 128, :], spread_side)
            if part == 0:
                got = jnp.where(top, got, 0.0)
            if part == 5:
                got = jnp.where(bottom, got, 0.0)
            got = got.astype(BF16)
            for y in range(4):
                for wx in range(4):
                    to = (part * 4 + y) * 128 + wx * 32
                    field[to:to + 32, :] = got[y * 32:y * 32 + 32, wx * 128:wx * 128 + 128]

    for r in range(12):
        both = (fine[2 * r * 128 + 32:2 * r * 128 + 96, :].astype(F32)
                + fine[(2 * r + 1) * 128 + 32:(2 * r + 1) * 128 + 96, :].astype(F32))
        mean = (both[0:16] + both[16:32] + both[32:48] + both[48:64]) * 0.125
        pool[r * 48:r * 48 + 16, :] = pltpu.roll(mean, 1, 1).astype(BF16)
        pool[r * 48 + 16:r * 48 + 32, :] = mean.astype(BF16)
        pool[r * 48 + 32:r * 48 + 48, :] = pltpu.roll(mean, 127, 1).astype(BF16)

    lane = iota((32, 128), 1)
    inside = ((lane >= 2) | ((lane == 1) & first)) & ((lane <= 65) | ((lane == 66) & last))
    own = (iota((128, 128), 1) >= 2) & (iota((128, 128), 1) <= 65)
    blank = jnp.zeros((32, 128), BF16)
    for r in range(1, 11):
        pre = dot(w_pre[...], pool[(r - 1) * 48:(r + 2) * 48, :])
        sig = 1.0 / (1.0 + jnp.exp(-pre))
        back = dot(w_bwd[...], cot[(2 * r - 1) * 128:(2 * r + 3) * 128, :])
        grad_act = back[128:160].astype(BF16).astype(F32)
        slope = grad_act * (sig * (1.0 + pre * (1.0 - sig)))
        valid = inside
        if r == 1:
            valid = inside & top
        if r == 10:
            valid = inside & bottom
        for value, to in ((pre * sig, act), (slope, gpre)):
            value = jnp.where(valid, value, 0.0)
            at = (r - 1) * 128
            to[at:at + 32, :] = pltpu.roll(value, 1, 1).astype(BF16)
            to[at + 32:at + 64, :] = value.astype(BF16)
            to[at + 64:at + 96, :] = pltpu.roll(value, 127, 1).astype(BF16)
            to[at + 96:at + 128, :] = blank
        if 2 <= r <= 9:
            keep_gj[(r - 2) * 128:(r - 1) * 128, :] = back[0:128]

    def own_cot(r):
        a, b = 2 * r * 128, (2 * r + 1) * 128
        both = jnp.concatenate([cot[a + 32:a + 96, :], cot[b + 32:b + 96, :]], axis=0)
        return jnp.where(own, both.astype(F32), 0.0).astype(BF16)

    def lanes(parts):
        return jnp.concatenate(parts, axis=1)

    grad = jnp.zeros((128, 512), F32)
    grad_up = jnp.zeros((128, 384), F32)
    grad_c = jnp.zeros((144, 32), F32)
    for r in range(2, 10, 2):
        lhs = lanes([own_cot(r), own_cot(r + 1)])
        grad += dot_nt(lhs, lanes([fine[(2 * q - 1) * 128:(2 * q + 3) * 128, :] for q in (r, r + 1)]))
        grad_up += dot_nt(lhs, lanes([act[(q - 2) * 128:(q + 1) * 128, :] for q in (r, r + 1)]))
        mine = [jnp.where(own[0:32], gpre[(q - 1) * 128 + 32:(q - 1) * 128 + 64, :].astype(F32), 0.0).astype(BF16)
                for q in (r, r + 1)]
        grad_c += dot_nt(lanes([pool[(q - 1) * 48:(q + 2) * 48, :] for q in (r, r + 1)]), lanes(mine))
    dys = ((0, 1, 1), (1, 1, 2))
    taps = [jnp.concatenate([grad_c[t * 16:t * 16 + 16], jnp.zeros((16, 96), F32)], axis=1) for t in range(9)]
    none = jnp.zeros((16, 128), F32)
    for block in range(6):
        if block < 3:
            ky = block
            total = sum(grad[py * 64:py * 64 + 32, (ky + py) * 128:(ky + py + 1) * 128] for py in range(2))
            odd = sum(grad[py * 64 + 32:py * 64 + 64, (ky + py) * 128:(ky + py + 1) * 128] for py in range(2))
            total = total + pltpu.roll(odd, 96, 1)
        else:
            ky = block - 3
            even, odd = (sum(grad_up[py * 64 + px * 32:py * 64 + px * 32 + 32, dys[py][ky] * 128:(dys[py][ky] + 1) * 128]
                             for py in range(2)) for px in range(2))
            total = jnp.where(lane < 64, even, pltpu.roll(even, 32, 1)) + jnp.where(lane < 32, pltpu.roll(odd, 96, 1), odd)
        extra = jnp.concatenate([taps[t] if t < 9 else none for t in (2 * block, 2 * block + 1)], axis=0)
        sums[block * 32:block * 32 + 32, :] = jnp.where(lane < 96, total, pltpu.roll(extra, 96, 1))
    count, depth = sums_ref.shape[0], sums_ref.shape[1]
    for j in range(count):
        sums_ref[j] = sums[j * depth:(j + 1) * depth, :]

    joiner = iota((256, 128), 0)
    joiner = (2 * ((joiner & 127) - 2) + (joiner >> 7) == iota((256, 128), 1)).astype(F32).astype(BF16)

    def place(values, r):
        values = values.astype(BF16)
        for py in range(2):
            at = (2 * (r - 2) + py) * 32
            flat[at:at + 32, 0:128] = values[py * 64:py * 64 + 32]
            flat[at:at + 32, 128:256] = values[py * 64 + 32:py * 64 + 64]

    def finish(to):
        for part in range(4):
            joined = dot(flat[part * 128:part * 128 + 128, :], joiner)
            for j in range(8):
                turn[pl.ds(part * 8 + j, 16, stride=32), :] = joined[j * 16:j * 16 + 16]
        to[...] = turn[...].astype(BF16)

    for r in range(2, 10):
        got = dot(w_fwd[:, 0:512], fine[(2 * r - 1) * 128:(2 * r + 3) * 128, :])
        got += dot(w_fwd[:, 512:896], act[(r - 2) * 128:(r + 1) * 128, :])
        place(got, r)
    finish(out_ref)
    for r in range(2, 10):
        low = dot(w_gp[...], gpre[(r - 2) * 128:(r + 1) * 128, :]).astype(BF16).astype(F32) * 0.125
        place(keep_gj[(r - 2) * 128:(r - 1) * 128, :] + jnp.concatenate([low] * 8, axis=0), r)
    finish(gf_ref)


def sum_kernel(n_wide, n_narrow, scale_fine, scale_coarse, sums_ref, gfine_ref, gcoarse_ref,
               got1, part, got2, fin, turn, send1, recv1, send2, recv2, send3, recv3):
    g1, g2 = n_narrow * OUTER, n_wide // OUTER
    depth = ROWS // g1
    me_y, me_x = lax.axis_index("wide"), lax.axis_index("narrow")
    me1 = lax.div(me_y, g2) * n_narrow + me_x
    me2 = lax.rem(me_y, g2)

    def first(k):
        return (lax.div(k, n_narrow) * g2 + me2, lax.rem(k, n_narrow))

    def second(k):
        return (lax.div(me_y, g2) * g2 + k, me_x)

    barrier = pltpu.get_barrier_semaphore()

    @pl.loop(1, g1)
    def _(d):
        pl.semaphore_signal(barrier, inc=1, device_id=first(lax.rem(me1 + d, g1)), device_id_type=MESH)

    @pl.loop(1, g2)
    def _(d):
        pl.semaphore_signal(barrier, inc=1, device_id=second(lax.rem(me2 + d, g2)), device_id_type=MESH)

    pl.semaphore_wait(barrier, g1 + g2 - 2)

    def copy1(d):
        to = lax.rem(me1 + d, g1)
        return pltpu.make_async_remote_copy(
            src_ref=sums_ref.at[to], dst_ref=got1.at[d], send_sem=send1.at[d], recv_sem=recv1.at[d],
            device_id=first(to), device_id_type=MESH)

    def copy2(d, slot):
        return pltpu.make_async_remote_copy(
            src_ref=part, dst_ref=got2.at[slot], send_sem=send2.at[d], recv_sem=recv2.at[slot],
            device_id=second(lax.rem(me2 + d, g2)), device_id_type=MESH)

    def copy3(d, slot):
        return pltpu.make_async_remote_copy(
            src_ref=fin.at[me1], dst_ref=fin.at[slot], send_sem=send3.at[d], recv_sem=recv3.at[slot],
            device_id=first(lax.rem(me1 + d, g1)), device_id_type=MESH)

    def run(count, body):
        @pl.loop(1, count)
        def _(d):
            body(d)

    run(g1, lambda d: copy1(d).start())
    run(g1, lambda d: copy1(d).wait_recv())
    total = sums_ref[me1]
    for d in range(1, g1):
        total += got1[d]
    part[...] = total
    run(g2, lambda d: copy2(d, me2).start())
    got2[me2] = total
    run(g2, lambda d: copy2(d, lax.rem(me2 + d, g2)).wait_recv())
    total = got2[0]
    for k in range(1, g2):
        total += got2[k]
    fin[me1] = total
    run(g1, lambda d: copy3(d, me1).start())
    run(g1, lambda d: copy3(d, lax.rem(me1 + d, g1)).wait_recv())
    for j in range(g1):
        turn[j * depth:(j + 1) * depth, :] = fin[j]
    lane = iota((16, 128), 1)
    for ky in range(3):
        flow = [turn[ky * 32 + z * 16:ky * 32 + z * 16 + 16, :] for z in range(2)]
        rise = [turn[96 + ky * 32 + z * 16:96 + ky * 32 + z * 16 + 16, :] for z in range(2)]
        ups = (rise[1], rise[0] + rise[1], rise[0])
        for kx in range(3):
            near0 = [pltpu.roll(flow[z], (-32 * kx) % 128, 1) if kx else flow[z] for z in range(2)]
            near1 = [pltpu.roll(flow[z], (-32 * kx - 16) % 128, 1) for z in range(2)]
            own = (near0[1], near0[0] + near1[1], near1[0])
            for kz in range(3):
                whole = jnp.where(lane < 16, own[kz], pltpu.roll(ups[kz], (16 - 32 * kx) % 128, 1))
                at = ((ky * 3 + kz) * 3 + kx) * 16
                gfine_ref[at:at + 16, :] = (whole * scale_fine)[:, 0:48]
                if kz == 1:
                    t = ky * 3 + kx
                    row = (t // 2) * 32 + (t % 2) * 16
                    coarse = pltpu.roll(turn[row:row + 16, :], 32, 1)[:, 0:32] * scale_coarse
                    gcoarse_ref[at:at + 16, :] = coarse
                else:
                    gcoarse_ref[at:at + 16, :] = jnp.zeros((16, 32), F32)
    run(g1, lambda d: copy1(d).wait_send())
    run(g2, lambda d: copy2(d, me2).wait_send())
    run(g1, lambda d: copy3(d, me1).wait_send())


def shards(n_wide, n_narrow, features, cotangent, coarse_weight, fine_weight):
    inside = pl.BlockSpec(memory_space=VMEM)
    shape = jax.ShapeDtypeStruct
    g1, g2 = n_narrow * OUTER, n_wide // OUTER
    depth = ROWS // g1
    cells = n_wide * 16 * 2 * n_narrow * 128
    fw = jnp.transpose(fine_weight, (2, 3, 4, 0, 1)).reshape(432, 48)
    cw = jnp.transpose(coarse_weight, (2, 3, 4, 1, 0)).reshape(432, 32)
    dma = pltpu.SemaphoreType.DMA
    ext, left, right = pl.pallas_call(
        functools.partial(halo_kernel, n_wide, n_narrow),
        out_shape=(shape((2, 768, 128), BF16), shape((16, 768), BF16), shape((16, 768), BF16)),
        in_specs=[inside] * 2,
        out_specs=(inside,) * 3,
        scratch_shapes=[VMEM((2, 512, 128), F32), VMEM((16, 512), BF16), VMEM((16, 512), BF16), dma((8,)), dma((8,))],
        compiler_params=pltpu.CompilerParams(collective_id=0, has_side_effects=True),
        name="halo",
    )(features.reshape(512, 128), cotangent.reshape(512, 128))
    output, grad_features, sums = pl.pallas_call(
        functools.partial(level_kernel, n_wide, n_narrow),
        out_shape=(shape((512, 128), BF16), shape((512, 128), BF16), shape((g1, depth, 128), F32)),
        in_specs=[inside] * 5,
        out_specs=(inside,) * 3,
        scratch_shapes=[
            VMEM((864, 128), F32), VMEM((768, 128), BF16), VMEM((128, 896), BF16), VMEM((160, 512), BF16),
            VMEM((144, 128), BF16), VMEM((32, 144), BF16), VMEM((16, 384), BF16),
            VMEM((3072, 128), BF16), VMEM((3072, 128), BF16), VMEM((576, 128), BF16),
            VMEM((1280, 128), BF16), VMEM((1280, 128), BF16), VMEM((1024, 128), F32),
            VMEM((512, 256), BF16), VMEM((512, 128), F32), VMEM((ROWS, 128), F32),
        ],
        compiler_params=pltpu.CompilerParams(vmem_limit_bytes=40 * 1024 * 1024),
        name="level",
    )(ext, left, right, fw, cw)
    gfine, gcoarse = pl.pallas_call(
        functools.partial(sum_kernel, n_wide, n_narrow, 1.0 / math.sqrt(cells), 1.0 / math.sqrt(cells // 8)),
        out_shape=(shape((432, 48), F32), shape((432, 32), F32)),
        in_specs=[inside],
        out_specs=(inside,) * 2,
        scratch_shapes=[
            VMEM((g1, depth, 128), F32), VMEM((depth, 128), F32), VMEM((g2, depth, 128), F32),
            VMEM((g1, depth, 128), F32), VMEM((ROWS, 128), F32),
            dma((g1,)), dma((g1,)), dma((g2,)), dma((g2,)), dma((g1,)), dma((g1,)),
        ],
        compiler_params=pltpu.CompilerParams(collective_id=1, has_side_effects=True),
        name="sums",
    )(sums)
    return (
        output.reshape(16, 16, 2, 128),
        grad_features.reshape(16, 16, 2, 128),
        jnp.transpose(gfine.reshape(3, 3, 3, 16, 48), (3, 4, 0, 1, 2)),
        jnp.transpose(gcoarse.reshape(3, 3, 3, 16, 32), (4, 3, 0, 1, 2)),
    )


def solution(mesh):
    placed = P(None, "wide", None, "narrow")
    return jax.shard_map(
        functools.partial(shards, mesh.shape["wide"], mesh.shape["narrow"]),
        mesh=mesh,
        in_specs=(placed, placed, P(), P()),
        out_specs=(placed, placed, P(), P()),
        check_vma=False,
    )
```

time: 648 us -> 63.1 us (0.10); the launches traced: 639 us -> 62.8 us
  waiting for transfers between devices: 302 us -> 0 us
  blocking collectives: 106 us -> 0 us
  starting transfers between devices: 90.7 us -> 0 us
  Pallas kernels: 0 us -> 56.6 us
  local copies, waits for them, and re-layouts: 56.7 us -> 5.49 us
  matrix products: 50.9 us -> 0 us
  other arithmetic: 18 us -> 0 us
  between operations: 14.9 us -> 0.7 us
    psum x1 -> x0, waiting for transfers between devices: 293 us -> none  [shards(): lax.psum((local_fine, local_coarse), ('wide', 'narrow'))]
    psum x1 -> x0, blocking collectives: 106 us -> none  [shards(): lax.psum((local_fine, local_coarse), ('wide', 'narrow'))]
    pallas_call x0 -> x3, Pallas kernels: none -> 56.6 us  [the longest x1 30 us: shards(): pl.pallas_call(functools.partial(sum_kernel, n_wide, n_narrow, 1.0 / math...]
    ppermute x12 -> x0, starting transfers between devices: 55.3 us -> none  [the longest x6 27.7 us: extended_2(): before = lax.ppermute(last, axis, up)]
    transpose x2 -> x0, matrix products: 37 us -> none  [weight_grad(): return jnp.transpose(result, (1, 0, 2, 3, 4))]
    all_to_all x4 -> x0, starting transfers between devices: 35.3 us -> none  [the longest x2 20.8 us: into_coarse(): lax.all_to_all(shortened(field), 'narrow', split_axis=1, concat_axis=3, t...]
    conv_general_dilated x19 -> x0, local copies, waits for them, and re-layouts: 23.1 us -> none  [correlate(): lax.conv_general_dilated(padded[None], kernel, (1, 1, 1), 'VALID', dimens...]
    broadcast_in_dim x11 -> x0, local copies, waits for them, and re-layouts: 17.2 us -> none  [the longest x2 10.8 us: weight_grad(): padded[:, None]]
  transfers between devices with their start and end apart: 17 -> 0, of which waited for: 4 -> 0; matrix products, arithmetic and copies ran while one was open for 10% -> 0% of each run, Pallas kernels for 0% -> 0%
where the time goes in v1:
time: 63.1 us; the launch traced here: 62.8 us
  Pallas kernels  56.6 us (90%)
  local copies, waits for them, and re-layouts  5.49 us (9%)
  between operations  0.7 us (1%)
    pallas_call x1, Pallas kernels, shards(): pl.pallas_call(functools.partial(sum_kernel, n_wide, n_narrow, 1.0 / math...  30 us
    pallas_call x1, Pallas kernels, shards(): pl.pallas_call(functools.partial(halo_kernel, n_wide, n_narrow), out_shap...  22.5 us
    unnamed x16, local copies, waits for them, and re-layouts  5.49 us
    pallas_call x1, Pallas kernels, shards(): pl.pallas_call(functools.partial(level_kernel, n_wide, n_narrow), out_sha...  4.09 us

profile of v1, /device:TPU:1, one launch (start us, length us, event | category | flops | bytes accessed | tf_op | source)
XLA Modules:
  0.0 62.8 jit_solution(6423676391535885850)
XLA Ops:
  0.6 0.0 copy-start.2
  0.6 0.0 copy-start.3
  0.7 22.5 %halo.1 = (bf16[2,768,128]{2,1,0:T(8,128)(2,1)}, bf16[16,768]{1,0:T(8,128)(2,1)}, bf16[16,768]{1,0:T(8,128)(2,1)}) custom-call(bf16[512,128]{1,0:T(8,128)(2,1)} %bitcast.20, bf16[512,128]{1,0:T(8,128)(2,1)} %bitcast.21), custom_call_target="tpu_custom_call" | custom-call | tf_op jit(solution)/shard_map/halo/pallas_call | solution.py:390
  23.2 0.0 copy-done.2
  23.2 0.0 copy-done.3
  23.2 0.0 copy-start
  23.2 1.0 %copy-done = bf16[2,768,128]{2,1,0:T(8,128)(2,1)S(1)} copy-done((bf16[2,768,128]{2,1,0:T(8,128)(2,1)S(1)}, bf16[2,768,128]{2,1,0:T(8,128)(2,1)}, u32[]{:S(2)}) %copy-start) | copy-done | bytes 393240
  24.2 0.0 copy-start.4
  24.2 0.7 %copy-done.4 = bf16[16,768]{1,0:T(8,128)(2,1)S(1)} copy-done((bf16[16,768]{1,0:T(8,128)(2,1)S(1)}, bf16[16,768]{1,0:T(8,128)(2,1)}, u32[]{:S(2)}) %copy-start.4) | copy-done | bytes 24600
  24.9 0.0 copy-start.5
  24.9 0.7 %copy-done.5 = bf16[16,768]{1,0:T(8,128)(2,1)S(1)} copy-done((bf16[16,768]{1,0:T(8,128)(2,1)S(1)}, bf16[16,768]{1,0:T(8,128)(2,1)}, u32[]{:S(2)}) %copy-start.5) | copy-done | bytes 24600
  25.7 4.1 %level.1 = (bf16[512,128]{1,0:T(8,128)(2,1)}, bf16[512,128]{1,0:T(8,128)(2,1)}, f32[32,6,128]{2,1,0:T(8,128)S(1)}) custom-call(bf16[2,768,128]{2,1,0:T(8,128)(2,1)S(1)} %copy-done, bf16[16,768]{1,0:T(8,128)(2,1)S(1)} %copy-done.4, bf16[16,768]{1,0:T(8,128)(2,1)S(1)} %copy-done.5, bf16[432,48]{1,0:T(8,128)(2,1)S(1)} %bitcast.16, bf16[432,32]{1,0:T(8,128)(2,1)S(1)} %bitcast.17), custom_call_target="tpu_custom_call" | custom-call | tf_op jit(solution)/shard_map/level/pallas_call | solution.py:399
  29.8 0.0 copy-start.1
  29.8 0.7 %copy-done.1 = f32[32,6,128]{2,1,0:T(8,128)} copy-done((f32[32,6,128]{2,1,0:T(8,128)}, f32[32,6,128]{2,1,0:T(8,128)S(1)}, u32[]{:S(2)}) %copy-start.1) | copy-done | bytes 98328
  30.4 30.0 %sums.1 = (f32[432,48]{1,0:T(8,128)}, f32[432,32]{1,0:T(8,128)}) custom-call(f32[32,6,128]{2,1,0:T(8,128)} %copy-done.1), custom_call_target="tpu_custom_call" | custom-call | tf_op jit(solution)/shard_map/sums/pallas_call | solution.py:414
  60.4 0.0 copy-start.6
  60.4 1.7 %copy.10 = f32[16,48,3,3,3]{1,0,4,3,2:T(8,128)} copy(f32[16,48,3,3,3]{1,0,4,3,2:T(8,128)} %bitcast.19) | data formatting | bytes 165888
  62.1 0.0 copy-done.6
  62.1 0.7 %copy.11 = f32[32,16,3,3,3]{0,1,4,3,2:T(8,128)} copy(f32[32,16,3,3,3]{0,1,4,3,2:T(8,128)S(1)} %bitcast.18) | data formatting | bytes 110592
Async XLA Ops:
  0.6 22.6 %copy-start.2 = (bf16[16,48,3,3,3]{1,0,4,3,2:T(8,128)(2,1)S(1)}, bf16[16,48,3,3,3]{1,0,4,3,2:T(8,128)(2,1)}, u32[]{:S(2)}) copy-start(bf16[16,48,3,3,3]{1,0,4,3,2:T(8,128)(2,1)} %param.7) | copy-start | bytes 124420
  0.6 22.6 %copy-start.3 = (bf16[32,16,3,3,3]{0,1,4,3,2:T(8,128)(2,1)S(1)}, bf16[32,16,3,3,3]{0,1,4,3,2:T(8,128)(2,1)}, u32[]{:S(2)}) copy-start(bf16[32,16,3,3,3]{0,1,4,3,2:T(8,128)(2,1)} %param.6) | copy-start | bytes 82948
  23.2 1.0 %copy-start = (bf16[2,768,128]{2,1,0:T(8,128)(2,1)S(1)}, bf16[2,768,128]{2,1,0:T(8,128)(2,1)}, u32[]{:S(2)}) copy-start(bf16[2,768,128]{2,1,0:T(8,128)(2,1)} %get-tuple-element.12.ext_ref) | copy-start | bytes 1179652
  24.2 0.7 %copy-start.4 = (bf16[16,768]{1,0:T(8,128)(2,1)S(1)}, bf16[16,768]{1,0:T(8,128)(2,1)}, u32[]{:S(2)}) copy-start(bf16[16,768]{1,0:T(8,128)(2,1)} %get-tuple-element.13.left_ref) | copy-start | bytes 73732
  24.9 0.7 %copy-start.5 = (bf16[16,768]{1,0:T(8,128)(2,1)S(1)}, bf16[16,768]{1,0:T(8,128)(2,1)}, u32[]{:S(2)}) copy-start(bf16[16,768]{1,0:T(8,128)(2,1)} %get-tuple-element.14.right_ref) | copy-start | bytes 73732
  29.8 0.7 %copy-start.1 = (f32[32,6,128]{2,1,0:T(8,128)}, f32[32,6,128]{2,1,0:T(8,128)S(1)}, u32[]{:S(2)}) copy-start(f32[32,6,128]{2,1,0:T(8,128)S(1)} %get-tuple-element.17.sums_ref) | copy-start | bytes 294916
  60.4 1.7 %copy-start.6 = (f32[432,32]{1,0:T(8,128)S(1)}, f32[432,32]{1,0:T(8,128)}, u32[]{:S(2)}) copy-start(f32[432,32]{1,0:T(8,128)} %get-tuple-element.19) | copy-start | bytes 165892

commit v2 on v1

--- a/solution.py
+++ b/solution.py
@@ -27,16 +27,14 @@
     return lax.broadcasted_iota(jnp.int32, shape, axis)
 
 
-def halo_kernel(n_wide, n_narrow, f_ref, c_ref, ext_ref, left_ref, right_ref,
-                wide32, go_left, go_right, send, recv):
-    me_y, me_x = lax.axis_index("wide"), lax.axis_index("narrow")
+def neighbours(n_wide, n_narrow, me_y, me_x):
     up, down = lax.rem(me_y + n_wide - 1, n_wide), lax.rem(me_y + 1, n_wide)
     west, east = lax.rem(me_x + n_narrow - 1, n_narrow), lax.rem(me_x + 1, n_narrow)
-    near = [(up, me_x), (down, me_x), (me_y, west), (me_y, east),
+    return [(up, me_x), (down, me_x), (me_y, west), (me_y, east),
             (up, west), (up, east), (down, west), (down, east)]
-    barrier = pltpu.get_barrier_semaphore()
-    for device in near:
-        pl.semaphore_signal(barrier, inc=1, device_id=device, device_id_type=MESH)
+
+
+def pack_own(f_ref, c_ref, ext_ref, wide32, go_left, go_right):
     for k, ref in enumerate((f_ref, c_ref)):
         wide32[k] = ref[...].astype(F32)
         for j in range(32):
@@ -49,7 +47,9 @@
             pick = (row >= 4 * k) & (row < 4 * k + 4) & (col == start + row - 4 * k)
             total += dot_nt(pick.astype(F32).astype(BF16), ext_ref[k, 128:640, :])
         buf[...] = total.astype(BF16)
-    pl.semaphore_wait(barrier, 8)
+
+
+def halo_copies(near, ext_ref, left_ref, right_ref, go_left, go_right, send, recv):
     plan = [
         (ext_ref.at[:, pl.ds(128, 128), :], ext_ref.at[:, pl.ds(640, 128), :]),
         (ext_ref.at[:, pl.ds(512, 128), :], ext_ref.at[:, pl.ds(0, 128), :]),
@@ -60,14 +60,12 @@
         (go_left.at[:, pl.ds(384, 128)], right_ref.at[:, pl.ds(0, 128)]),
         (go_right.at[:, pl.ds(384, 128)], left_ref.at[:, pl.ds(0, 128)]),
     ]
-    copies = []
-    for j, (src, dst) in enumerate(plan):
-        copies.append(pltpu.make_async_remote_copy(
+    return [
+        pltpu.make_async_remote_copy(
             src_ref=src, dst_ref=dst, send_sem=send.at[j], recv_sem=recv.at[j],
-            device_id=near[j], device_id_type=MESH))
-        copies[-1].start()
-    for copy in copies:
-        copy.wait()
+            device_id=near[j], device_id_type=MESH)
+        for j, (src, dst) in enumerate(plan)
+    ]
 
 
 def prepare_weights(fw_ref, cw_ref, wide_w, stack, w_fwd, w_bwd, stack_c, w_pre, w_gp):
@@ -156,12 +154,8 @@
     w_pre[...] = dot_nt(eye[0:32], stack_c[...]).astype(BF16)
 
 
-def level_kernel(n_wide, n_narrow, ext_ref, left_ref, right_ref, fw_ref, cw_ref,
-                 out_ref, gf_ref, sums_ref,
-                 wide_w, stack, w_fwd, w_bwd, stack_c, w_pre, w_gp,
-                 fine, cot, pool, act, gpre, keep_gj, flat, turn, sums):
-    me_y, me_x = lax.axis_index("wide"), lax.axis_index("narrow")
-    prepare_weights(fw_ref, cw_ref, wide_w, stack, w_fwd, w_bwd, stack_c, w_pre, w_gp)
+def level_gradients(n_wide, n_narrow, me_y, me_x, ext_ref, left_ref, right_ref, sums_ref,
+                    w_bwd, w_pre, fine, cot, pool, act, gpre, keep_gj, sums):
     top, bottom = me_y > 0, me_y < n_wide - 1
     first, last = me_x > 0, me_x < n_narrow - 1
 
@@ -261,6 +255,8 @@
     for j in range(count):
         sums_ref[j] = sums[j * depth:(j + 1) * depth, :]
 
+
+def level_outputs(out_ref, gf_ref, w_fwd, w_gp, fine, act, gpre, keep_gj, flat, turn):
     joiner = iota((256, 128), 0)
     joiner = (2 * ((joiner & 127) - 2) + (joiner >> 7) == iota((256, 128), 1)).astype(F32).astype(BF16)
 
@@ -289,36 +285,53 @@
     finish(gf_ref)
 
 
-def sum_kernel(n_wide, n_narrow, scale_fine, scale_coarse, sums_ref, gfine_ref, gcoarse_ref,
-               got1, part, got2, fin, turn, send1, recv1, send2, recv2, send3, recv3):
-    g1, g2 = n_narrow * OUTER, n_wide // OUTER
+def main_kernel(n_wide, n_narrow, f_ref, c_ref, fw_ref, cw_ref, out_hbm, gf_hbm, total_ref,
+                wide32, go_left, go_right, ext, left, right, halo_send, halo_recv,
+                wide_w, stack, w_fwd, w_bwd, stack_c, w_pre, w_gp,
+                fine, cot, pool, act, gpre, keep_gj, flat, turn, sums,
+                out_v, gf_v, out_sem, mine, got1, part, got2, fin, send1, recv1, send2, recv2, send3, recv3):
+    g1, g2 = n_wide // OUTER, n_narrow * OUTER
     depth = ROWS // g1
     me_y, me_x = lax.axis_index("wide"), lax.axis_index("narrow")
-    me1 = lax.div(me_y, g2) * n_narrow + me_x
-    me2 = lax.rem(me_y, g2)
+    me1 = lax.rem(me_y, g1)
+    me2 = lax.div(me_y, g1) * n_narrow + me_x
 
     def first(k):
-        return (lax.div(k, n_narrow) * g2 + me2, lax.rem(k, n_narrow))
+        return (me_y - me1 + k, me_x)
 
     def second(k):
-        return (lax.div(me_y, g2) * g2 + k, me_x)
+        return (lax.div(k, n_narrow) * g1 + me1, lax.rem(k, n_narrow))
+
+    def run(count, body):
+        @pl.loop(1, count)
+        def _(d):
+            body(d)
 
     barrier = pltpu.get_barrier_semaphore()
-
-    @pl.loop(1, g1)
-    def _(d):
-        pl.semaphore_signal(barrier, inc=1, device_id=first(lax.rem(me1 + d, g1)), device_id_type=MESH)
-
-    @pl.loop(1, g2)
-    def _(d):
-        pl.semaphore_signal(barrier, inc=1, device_id=second(lax.rem(me2 + d, g2)), device_id_type=MESH)
-
-    pl.semaphore_wait(barrier, g1 + g2 - 2)
+    near = neighbours(n_wide, n_narrow, me_y, me_x)
+
+    def greet(device):
+        pl.semaphore_signal(barrier, inc=1, device_id=device, device_id_type=MESH)
+
+    for device in near:
+        greet(device)
+    run(g2, lambda d: greet(second(lax.rem(me2 + d, g2))))
+    run(g1, lambda d: greet(first(lax.rem(me1 + d, g1))))
+    pack_own(f_ref, c_ref, ext, wide32, go_left, go_right)
+    prepare_weights(fw_ref, cw_ref, wide_w, stack, w_fwd, w_bwd, stack_c, w_pre, w_gp)
+    pl.semaphore_wait(barrier, 8 + g1 + g2 - 2)
+    halo = halo_copies(near, ext, left, right, go_left, go_right, halo_send, halo_recv)
+    for copy in halo:
+        copy.start()
+    for copy in halo:
+        copy.wait_recv()
+    level_gradients(n_wide, n_narrow, me_y, me_x, ext, left, right, mine,
+                    w_bwd, w_pre, fine, cot, pool, act, gpre, keep_gj, sums)
 
     def copy1(d):
         to = lax.rem(me1 + d, g1)
         return pltpu.make_async_remote_copy(
-            src_ref=sums_ref.at[to], dst_ref=got1.at[d], send_sem=send1.at[d], recv_sem=recv1.at[d],
+            src_ref=mine.at[to], dst_ref=got1.at[d], send_sem=send1.at[d], recv_sem=recv1.at[d],
             device_id=first(to), device_id_type=MESH)
 
     def copy2(d, slot):
@@ -331,14 +344,13 @@
             src_ref=fin.at[me1], dst_ref=fin.at[slot], send_sem=send3.at[d], recv_sem=recv3.at[slot],
             device_id=first(lax.rem(me1 + d, g1)), device_id_type=MESH)
 
-    def run(count, body):
-        @pl.loop(1, count)
-        def _(d):
-            body(d)
-
     run(g1, lambda d: copy1(d).start())
+    level_outputs(out_v, gf_v, w_fwd, w_gp, fine, act, gpre, keep_gj, flat, turn)
+    writes = [pltpu.make_async_copy(out_v, out_hbm, out_sem.at[0]), pltpu.make_async_copy(gf_v, gf_hbm, out_sem.at[1])]
+    for write in writes:
+        write.start()
     run(g1, lambda d: copy1(d).wait_recv())
-    total = sums_ref[me1]
+    total = mine[me1]
     for d in range(1, g1):
         total += got1[d]
     part[...] = total
@@ -350,9 +362,22 @@
         total += got2[k]
     fin[me1] = total
     run(g1, lambda d: copy3(d, me1).start())
+    for copy in halo:
+        copy.wait_send()
+    for write in writes:
+        write.wait()
+    run(g1, lambda d: copy1(d).wait_send())
+    run(g2, lambda d: copy2(d, me2).wait_send())
     run(g1, lambda d: copy3(d, lax.rem(me1 + d, g1)).wait_recv())
     for j in range(g1):
-        turn[j * depth:(j + 1) * depth, :] = fin[j]
+        total_ref[j * depth:(j + 1) * depth, :] = fin[j]
+    run(g1, lambda d: copy3(d, me1).wait_send())
+
+
+def finish_kernel(scale_fine, scale_coarse, turn, out_in, gf_in, gfine_ref, gcoarse_ref, out_ref, gf_ref, sem):
+    copies = [pltpu.make_async_copy(out_in, out_ref, sem.at[0]), pltpu.make_async_copy(gf_in, gf_ref, sem.at[1])]
+    for copy in copies:
+        copy.start()
     lane = iota((16, 128), 1)
     for ky in range(3):
         flow = [turn[ky * 32 + z * 16:ky * 32 + z * 16 + 16, :] for z in range(2)]
@@ -373,57 +398,50 @@
                     gcoarse_ref[at:at + 16, :] = coarse
                 else:
                     gcoarse_ref[at:at + 16, :] = jnp.zeros((16, 32), F32)
-    run(g1, lambda d: copy1(d).wait_send())
-    run(g2, lambda d: copy2(d, me2).wait_send())
-    run(g1, lambda d: copy3(d, me1).wait_send())
+    for copy in copies:
+        copy.wait()
 
 
 def shards(n_wide, n_narrow, features, cotangent, coarse_weight, fine_weight):
     inside = pl.BlockSpec(memory_space=VMEM)
     shape = jax.ShapeDtypeStruct
-    g1, g2 = n_narrow * OUTER, n_wide // OUTER
+    g1, g2 = n_wide // OUTER, n_narrow * OUTER
     depth = ROWS // g1
     cells = n_wide * 16 * 2 * n_narrow * 128
     fw = jnp.transpose(fine_weight, (2, 3, 4, 0, 1)).reshape(432, 48)
     cw = jnp.transpose(coarse_weight, (2, 3, 4, 1, 0)).reshape(432, 32)
     dma = pltpu.SemaphoreType.DMA
-    ext, left, right = pl.pallas_call(
-        functools.partial(halo_kernel, n_wide, n_narrow),
-        out_shape=(shape((2, 768, 128), BF16), shape((16, 768), BF16), shape((16, 768), BF16)),
-        in_specs=[inside] * 2,
-        out_specs=(inside,) * 3,
-        scratch_shapes=[VMEM((2, 512, 128), F32), VMEM((16, 512), BF16), VMEM((16, 512), BF16), dma((8,)), dma((8,))],
-        compiler_params=pltpu.CompilerParams(collective_id=0, has_side_effects=True),
-        name="halo",
-    )(features.reshape(512, 128), cotangent.reshape(512, 128))
+    large = pl.BlockSpec(memory_space=pl.ANY)
     output, grad_features, sums = pl.pallas_call(
-        functools.partial(level_kernel, n_wide, n_narrow),
-        out_shape=(shape((512, 128), BF16), shape((512, 128), BF16), shape((g1, depth, 128), F32)),
-        in_specs=[inside] * 5,
-        out_specs=(inside,) * 3,
+        functools.partial(main_kernel, n_wide, n_narrow),
+        out_shape=(shape((512, 128), BF16), shape((512, 128), BF16), shape((ROWS, 128), F32)),
+        in_specs=[inside] * 4,
+        out_specs=(large, large, inside),
         scratch_shapes=[
+            VMEM((2, 512, 128), F32), VMEM((16, 512), BF16), VMEM((16, 512), BF16),
+            VMEM((2, 768, 128), BF16), VMEM((16, 768), BF16), VMEM((16, 768), BF16), dma((8,)), dma((8,)),
             VMEM((864, 128), F32), VMEM((768, 128), BF16), VMEM((128, 896), BF16), VMEM((160, 512), BF16),
             VMEM((144, 128), BF16), VMEM((32, 144), BF16), VMEM((16, 384), BF16),
             VMEM((3072, 128), BF16), VMEM((3072, 128), BF16), VMEM((576, 128), BF16),
             VMEM((1280, 128), BF16), VMEM((1280, 128), BF16), VMEM((1024, 128), F32),
             VMEM((512, 256), BF16), VMEM((512, 128), F32), VMEM((ROWS, 128), F32),
-        ],
-        compiler_params=pltpu.CompilerParams(vmem_limit_bytes=40 * 1024 * 1024),
-        name="level",
-    )(ext, left, right, fw, cw)
-    gfine, gcoarse = pl.pallas_call(
-        functools.partial(sum_kernel, n_wide, n_narrow, 1.0 / math.sqrt(cells), 1.0 / math.sqrt(cells // 8)),
-        out_shape=(shape((432, 48), F32), shape((432, 32), F32)),
-        in_specs=[inside],
-        out_specs=(inside,) * 2,
-        scratch_shapes=[
-            VMEM((g1, depth, 128), F32), VMEM((depth, 128), F32), VMEM((g2, depth, 128), F32),
-            VMEM((g1, depth, 128), F32), VMEM((ROWS, 128), F32),
+            VMEM((512, 128), BF16), VMEM((512, 128), BF16), dma((2,)),
+            VMEM((g1, depth, 128), F32), VMEM((g1, depth, 128), F32), VMEM((depth, 128), F32),
+            VMEM((g2, depth, 128), F32), VMEM((g1, depth, 128), F32),
             dma((g1,)), dma((g1,)), dma((g2,)), dma((g2,)), dma((g1,)), dma((g1,)),
         ],
-        compiler_params=pltpu.CompilerParams(collective_id=1, has_side_effects=True),
-        name="sums",
-    )(sums)
+        compiler_params=pltpu.CompilerParams(
+            collective_id=0, has_side_effects=True, vmem_limit_bytes=40 * 1024 * 1024),
+        name="levels",
+    )(features.reshape(512, 128), cotangent.reshape(512, 128), fw, cw)
+    gfine, gcoarse, output, grad_features = pl.pallas_call(
+        functools.partial(finish_kernel, 1.0 / math.sqrt(cells), 1.0 / math.sqrt(cells // 8)),
+        out_shape=(shape((432, 48), F32), shape((432, 32), F32), shape((512, 128), BF16), shape((512, 128), BF16)),
+        in_specs=[inside, large, large],
+        out_specs=(inside, inside, large, large),
+        scratch_shapes=[dma((2,))],
+        name="finish",
+    )(sums, output, grad_features)
     return (
         output.reshape(16, 16, 2, 128),
         grad_features.reshape(16, 16, 2, 128),

time: 63.1 us -> 61.8 us (0.979)
  Pallas kernels: 56.6 us -> 55.3 us
    pallas_call x3 -> x2, Pallas kernels: 56.6 us -> 55.3 us  [the longest x1 44.6 us: shards(): pl.pallas_call(functools.partial(main_kernel, n_wide, n_narrow), out_shap...]
    unnamed x16 -> x14, local copies, waits for them, and re-layouts: 5.49 us -> 5.53 us
where the time goes in v2:
time: 61.8 us; the launch traced here: 61.5 us
  Pallas kernels  55.3 us (89%)
  local copies, waits for them, and re-layouts  5.53 us (9%)
  between operations  0.66 us (1%)
    pallas_call x1, Pallas kernels, shards(): pl.pallas_call(functools.partial(main_kernel, n_wide, n_narrow), out_shap...  44.6 us
    pallas_call x1, Pallas kernels, shards(): pl.pallas_call(functools.partial(finish_kernel, 1.0 / math.sqrt(cells), 1...  10.7 us
    unnamed x14, local copies, waits for them, and re-layouts  5.53 us

profile of v2, /device:TPU:1, one launch (start us, length us, event | category | flops | bytes accessed | tf_op | source)
XLA Modules:
  0.0 61.5 jit_solution(8076223740596639802)
XLA Ops:
  0.6 0.0 copy-start
  0.6 0.9 %copy-done = bf16[16,16,2,128]{3,2,1,0:T(2,128)(2,1)S(1)} copy-done((bf16[16,16,2,128]{3,2,1,0:T(2,128)(2,1)S(1)}, bf16[16,16,2,128]{3,2,1,0:T(2,128)(2,1)}, u32[]{:S(2)}) %copy-start) | copy-done | bytes 131096
  1.5 0.0 copy-start.1
  1.5 0.9 %copy-done.1 = bf16[16,16,2,128]{3,2,1,0:T(2,128)(2,1)S(1)} copy-done((bf16[16,16,2,128]{3,2,1,0:T(2,128)(2,1)S(1)}, bf16[16,16,2,128]{3,2,1,0:T(2,128)(2,1)}, u32[]{:S(2)}) %copy-start.1) | copy-done | bytes 131096
  2.4 0.0 copy-start.4
  2.4 0.9 %copy-done.4 = bf16[16,48,3,3,3]{1,0,4,3,2:T(8,128)(2,1)S(1)} copy-done((bf16[16,48,3,3,3]{1,0,4,3,2:T(8,128)(2,1)S(1)}, bf16[16,48,3,3,3]{1,0,4,3,2:T(8,128)(2,1)}, u32[]{:S(2)}) %copy-start.4) | copy-done | bytes 41496
  3.3 0.0 copy-start.5
  3.3 0.9 %copy-done.5 = bf16[32,16,3,3,3]{0,1,4,3,2:T(8,128)(2,1)S(1)} copy-done((bf16[32,16,3,3,3]{0,1,4,3,2:T(8,128)(2,1)S(1)}, bf16[32,16,3,3,3]{0,1,4,3,2:T(8,128)(2,1)}, u32[]{:S(2)}) %copy-start.5) | copy-done | bytes 27672
  4.2 44.6 %levels.1 = (bf16[512,128]{1,0:T(8,128)(2,1)S(1)}, bf16[512,128]{1,0:T(8,128)(2,1)S(1)}, f32[192,128]{1,0:T(8,128)S(1)}) custom-call(bf16[512,128]{1,0:T(8,128)(2,1)S(1)} %bitcast.16, bf16[512,128]{1,0:T(8,128)(2,1)S(1)} %bitcast.17, bf16[432,48]{1,0:T(8,128)(2,1)S(1)} %bitcast.18, bf16[432,32]{1,0:T(8,128)(2,1)S(1)} %bitcast.19), custom_call_target="tpu_custom_call" | custom-call | tf_op jit(solution)/shard_map/levels/pallas_call | solution.py:415
  48.9 0.0 copy-start.2
  48.9 0.6 %copy-done.2 = bf16[512,128]{1,0:T(8,128)(2,1)} copy-done((bf16[512,128]{1,0:T(8,128)(2,1)}, bf16[512,128]{1,0:T(8,128)(2,1)S(1)}, u32[]{:S(2)}) %copy-start.2) | copy-done | bytes 131096
  49.5 0.0 copy-start.3
  49.5 0.7 %copy-done.3 = bf16[512,128]{1,0:T(8,128)(2,1)} copy-done((bf16[512,128]{1,0:T(8,128)(2,1)}, bf16[512,128]{1,0:T(8,128)(2,1)S(1)}, u32[]{:S(2)}) %copy-start.3) | copy-done | bytes 131096
  50.2 0.0 copy-start.6
  50.2 0.6 %copy-done.6 = f32[192,128]{1,0:T(8,128)} copy-done((f32[192,128]{1,0:T(8,128)}, f32[192,128]{1,0:T(8,128)S(1)}, u32[]{:S(2)}) %copy-start.6) | copy-done | bytes 98328
  50.8 10.7 %finish.1 = (f32[432,48]{1,0:T(8,128)}, f32[432,32]{1,0:T(8,128)}, bf16[512,128]{1,0:T(8,128)(2,1)}, bf16[512,128]{1,0:T(8,128)(2,1)}) custom-call(f32[192,128]{1,0:T(8,128)} %copy-done.6, bf16[512,128]{1,0:T(8,128)(2,1)} %copy-done.2, bf16[512,128]{1,0:T(8,128)(2,1)} %copy-done.3), custom_call_target="tpu_custom_call" | custom-call | tf_op jit(solution)/shard_map/finish/pallas_call | solution.py:437
Async XLA Ops:
  0.6 0.9 %copy-start = (bf16[16,16,2,128]{3,2,1,0:T(2,128)(2,1)S(1)}, bf16[16,16,2,128]{3,2,1,0:T(2,128)(2,1)}, u32[]{:S(2)}) copy-start(bf16[16,16,2,128]{3,2,1,0:T(2,128)(2,1)} %param.4) | copy-start | bytes 393220
  1.5 0.9 %copy-start.1 = (bf16[16,16,2,128]{3,2,1,0:T(2,128)(2,1)S(1)}, bf16[16,16,2,128]{3,2,1,0:T(2,128)(2,1)}, u32[]{:S(2)}) copy-start(bf16[16,16,2,128]{3,2,1,0:T(2,128)(2,1)} %param.5) | copy-start | bytes 393220
  2.4 0.9 %copy-start.4 = (bf16[16,48,3,3,3]{1,0,4,3,2:T(8,128)(2,1)S(1)}, bf16[16,48,3,3,3]{1,0,4,3,2:T(8,128)(2,1)}, u32[]{:S(2)}) copy-start(bf16[16,48,3,3,3]{1,0,4,3,2:T(8,128)(2,1)} %param.7) | copy-start | bytes 124420
  3.3 0.9 %copy-start.5 = (bf16[32,16,3,3,3]{0,1,4,3,2:T(8,128)(2,1)S(1)}, bf16[32,16,3,3,3]{0,1,4,3,2:T(8,128)(2,1)}, u32[]{:S(2)}) copy-start(bf16[32,16,3,3,3]{0,1,4,3,2:T(8,128)(2,1)} %param.6) | copy-start | bytes 82948
  48.9 0.7 %copy-start.2 = (bf16[512,128]{1,0:T(8,128)(2,1)}, bf16[512,128]{1,0:T(8,128)(2,1)S(1)}, u32[]{:S(2)}) copy-start(bf16[512,128]{1,0:T(8,128)(2,1)S(1)} %get-tuple-element.12.out_in) | copy-start | bytes 393220
  49.5 0.7 %copy-start.3 = (bf16[512,128]{1,0:T(8,128)(2,1)}, bf16[512,128]{1,0:T(8,128)(2,1)S(1)}, u32[]{:S(2)}) copy-start(bf16[512,128]{1,0:T(8,128)(2,1)S(1)} %get-tuple-element.13.gf_in) | copy-start | bytes 393220
  50.2 0.6 %copy-start.6 = (f32[192,128]{1,0:T(8,128)}, f32[192,128]{1,0:T(8,128)S(1)}, u32[]{:S(2)}) copy-start(f32[192,128]{1,0:T(8,128)S(1)} %get-tuple-element.11.turn) | copy-start | bytes 294916

commit v3 on v2

--- a/solution.py
+++ b/solution.py
@@ -285,93 +285,99 @@
     finish(gf_ref)
 
 
-def main_kernel(n_wide, n_narrow, f_ref, c_ref, fw_ref, cw_ref, out_hbm, gf_hbm, total_ref,
+def main_kernel(n_wide, n_narrow, f_hbm, c_hbm, fw_hbm, cw_hbm, out_hbm, gf_hbm, total_ref,
+                f_ref, c_ref, fw_ref, cw_ref, in_sem,
                 wide32, go_left, go_right, ext, left, right, halo_send, halo_recv,
                 wide_w, stack, w_fwd, w_bwd, stack_c, w_pre, w_gp,
                 fine, cot, pool, act, gpre, keep_gj, flat, turn, sums,
                 out_v, gf_v, out_sem, mine, got1, part, got2, fin, send1, recv1, send2, recv2, send3, recv3):
     g1, g2 = n_wide // OUTER, n_narrow * OUTER
     depth = ROWS // g1
+    len_y, len_z, len_x = g1 // 2, 2 * OUTER, n_narrow // 2
     me_y, me_x = lax.axis_index("wide"), lax.axis_index("narrow")
     me1 = lax.rem(me_y, g1)
-    me2 = lax.div(me_y, g1) * n_narrow + me_x
-
-    def first(k):
-        return (me_y - me1 + k, me_x)
-
-    def second(k):
-        return (lax.div(k, n_narrow) * g1 + me1, lax.rem(k, n_narrow))
-
-    def run(count, body):
-        @pl.loop(1, count)
-        def _(d):
-            body(d)
+    run_z = lax.div(me_y, g1)
+    at_y, at_core = lax.div(me1, 2), lax.rem(me1, 2)
+    at_z, at_x = lax.rem(me_x, 2) * OUTER + run_z, lax.div(me_x, 2)
+    me2 = at_x * len_z + at_z
+
+    def far_first(sizes):
+        steps = [(a, b) for a in range(sizes[0]) for b in range(sizes[1]) if a or b]
+        return sorted(steps, key=lambda s: -sum(min(k, n - k) for k, n in zip(s, sizes)))
+
+    first, second = [], []
+    for dy, dcore in far_first((len_y, 2)):
+        k = lax.rem(at_y + dy, len_y) * 2 + lax.rem(at_core + dcore, 2)
+        first.append((k, (run_z * g1 + k, me_x)))
+    for dz, dx in far_first((len_z, len_x)):
+        z, x = lax.rem(at_z + dz, len_z), lax.rem(at_x + dx, len_x)
+        second.append((x * len_z + z, (lax.rem(z, OUTER) * g1 + me1, x * 2 + lax.div(z, OUTER))))
 
     barrier = pltpu.get_barrier_semaphore()
     near = neighbours(n_wide, n_narrow, me_y, me_x)
-
-    def greet(device):
+    for device in near + [device for _, device in second + first]:
         pl.semaphore_signal(barrier, inc=1, device_id=device, device_id_type=MESH)
-
-    for device in near:
-        greet(device)
-    run(g2, lambda d: greet(second(lax.rem(me2 + d, g2))))
-    run(g1, lambda d: greet(first(lax.rem(me1 + d, g1))))
+    reads = [pltpu.make_async_copy(src, dst, in_sem.at[j]) for j, (src, dst) in enumerate(
+        ((f_hbm, f_ref), (c_hbm, c_ref), (fw_hbm, fw_ref), (cw_hbm, cw_ref)))]
+    for read in reads:
+        read.start()
+    for read in reads[:2]:
+        read.wait()
     pack_own(f_ref, c_ref, ext, wide32, go_left, go_right)
+    for read in reads[2:]:
+        read.wait()
     prepare_weights(fw_ref, cw_ref, wide_w, stack, w_fwd, w_bwd, stack_c, w_pre, w_gp)
     pl.semaphore_wait(barrier, 8 + g1 + g2 - 2)
     halo = halo_copies(near, ext, left, right, go_left, go_right, halo_send, halo_recv)
-    for copy in halo:
-        copy.start()
+    for j in (4, 5, 6, 7, 2, 3, 0, 1):
+        halo[j].start()
     for copy in halo:
         copy.wait_recv()
     level_gradients(n_wide, n_narrow, me_y, me_x, ext, left, right, mine,
                     w_bwd, w_pre, fine, cot, pool, act, gpre, keep_gj, sums)
 
-    def copy1(d):
-        to = lax.rem(me1 + d, g1)
+    def send_all(group, source, slot, sends, receives):
+        for j, (k, device) in enumerate(group):
+            pltpu.make_async_remote_copy(
+                src_ref=source(k), dst_ref=slot(j), send_sem=sends, recv_sem=receives,
+                device_id=device, device_id_type=MESH).start()
+
+    def all_of(ref, sends, receives):
         return pltpu.make_async_remote_copy(
-            src_ref=mine.at[to], dst_ref=got1.at[d], send_sem=send1.at[d], recv_sem=recv1.at[d],
-            device_id=first(to), device_id_type=MESH)
-
-    def copy2(d, slot):
-        return pltpu.make_async_remote_copy(
-            src_ref=part, dst_ref=got2.at[slot], send_sem=send2.at[d], recv_sem=recv2.at[slot],
-            device_id=second(lax.rem(me2 + d, g2)), device_id_type=MESH)
-
-    def copy3(d, slot):
-        return pltpu.make_async_remote_copy(
-            src_ref=fin.at[me1], dst_ref=fin.at[slot], send_sem=send3.at[d], recv_sem=recv3.at[slot],
-            device_id=first(lax.rem(me1 + d, g1)), device_id_type=MESH)
-
-    run(g1, lambda d: copy1(d).start())
+            src_ref=ref, dst_ref=ref, send_sem=sends, recv_sem=receives,
+            device_id=near[0], device_id_type=MESH)
+
+    one = all_of(got1, send1, recv1)
+    two = all_of(got2.at[pl.ds(0, g2 - 1)], send2, recv2)
+    three = all_of(fin.at[pl.ds(0, g1 - 1)], send3, recv3)
+    send_all(first, lambda k: mine.at[k], lambda j: got1.at[j], send1, recv1)
     level_outputs(out_v, gf_v, w_fwd, w_gp, fine, act, gpre, keep_gj, flat, turn)
     writes = [pltpu.make_async_copy(out_v, out_hbm, out_sem.at[0]), pltpu.make_async_copy(gf_v, gf_hbm, out_sem.at[1])]
     for write in writes:
         write.start()
-    run(g1, lambda d: copy1(d).wait_recv())
+    one.wait_recv()
     total = mine[me1]
-    for d in range(1, g1):
-        total += got1[d]
+    for j in range(g1 - 1):
+        total += got1[j]
     part[...] = total
-    run(g2, lambda d: copy2(d, me2).start())
+    send_all(second, lambda k: part, lambda j: got2.at[me2], send2, recv2)
     got2[me2] = total
-    run(g2, lambda d: copy2(d, lax.rem(me2 + d, g2)).wait_recv())
+    for copy in halo:
+        copy.wait_send()
+    one.wait_send()
+    for write in writes:
+        write.wait()
+    two.wait_recv()
     total = got2[0]
     for k in range(1, g2):
         total += got2[k]
     fin[me1] = total
-    run(g1, lambda d: copy3(d, me1).start())
-    for copy in halo:
-        copy.wait_send()
-    for write in writes:
-        write.wait()
-    run(g1, lambda d: copy1(d).wait_send())
-    run(g2, lambda d: copy2(d, me2).wait_send())
-    run(g1, lambda d: copy3(d, lax.rem(me1 + d, g1)).wait_recv())
+    send_all(first, lambda k: fin.at[me1], lambda j: fin.at[me1], send3, recv3)
+    two.wait_send()
+    three.wait_recv()
     for j in range(g1):
         total_ref[j * depth:(j + 1) * depth, :] = fin[j]
-    run(g1, lambda d: copy3(d, me1).wait_send())
+    three.wait_send()
 
 
 def finish_kernel(scale_fine, scale_coarse, turn, out_in, gf_in, gfine_ref, gcoarse_ref, out_ref, gf_ref, sem):
@@ -415,9 +421,10 @@
     output, grad_features, sums = pl.pallas_call(
         functools.partial(main_kernel, n_wide, n_narrow),
         out_shape=(shape((512, 128), BF16), shape((512, 128), BF16), shape((ROWS, 128), F32)),
-        in_specs=[inside] * 4,
+        in_specs=[large] * 4,
         out_specs=(large, large, inside),
         scratch_shapes=[
+            VMEM((512, 128), BF16), VMEM((512, 128), BF16), VMEM((432, 48), BF16), VMEM((432, 32), BF16), dma((4,)),
             VMEM((2, 512, 128), F32), VMEM((16, 512), BF16), VMEM((16, 512), BF16),
             VMEM((2, 768, 128), BF16), VMEM((16, 768), BF16), VMEM((16, 768), BF16), dma((8,)), dma((8,)),
             VMEM((864, 128), F32), VMEM((768, 128), BF16), VMEM((128, 896), BF16), VMEM((160, 512), BF16),
@@ -426,18 +433,18 @@
             VMEM((1280, 128), BF16), VMEM((1280, 128), BF16), VMEM((1024, 128), F32),
             VMEM((512, 256), BF16), VMEM((512, 128), F32), VMEM((ROWS, 128), F32),
             VMEM((512, 128), BF16), VMEM((512, 128), BF16), dma((2,)),
-            VMEM((g1, depth, 128), F32), VMEM((g1, depth, 128), F32), VMEM((depth, 128), F32),
+            VMEM((g1, depth, 128), F32), VMEM((g1 - 1, depth, 128), F32), VMEM((depth, 128), F32),
             VMEM((g2, depth, 128), F32), VMEM((g1, depth, 128), F32),
-            dma((g1,)), dma((g1,)), dma((g2,)), dma((g2,)), dma((g1,)), dma((g1,)),
+            dma, dma, dma, dma, dma, dma,
         ],
         compiler_params=pltpu.CompilerParams(
-            collective_id=0, has_side_effects=True, vmem_limit_bytes=40 * 1024 * 1024),
+            collective_id=0, has_side_effects=True, vmem_limit_bytes=56 * 1024 * 1024),
         name="levels",
     )(features.reshape(512, 128), cotangent.reshape(512, 128), fw, cw)
     gfine, gcoarse, output, grad_features = pl.pallas_call(
         functools.partial(finish_kernel, 1.0 / math.sqrt(cells), 1.0 / math.sqrt(cells // 8)),
         out_shape=(shape((432, 48), F32), shape((432, 32), F32), shape((512, 128), BF16), shape((512, 128), BF16)),
-        in_specs=[inside, large, large],
+        in_specs=[inside] * 3,
         out_specs=(inside, inside, large, large),
         scratch_shapes=[dma((2,))],
         name="finish",

time: 61.8 us -> 46.3 us (0.75)
  Pallas kernels: 55.3 us -> 45.5 us
  local copies, waits for them, and re-layouts: 5.53 us -> 0 us
    pallas_call x1, Pallas kernels: 10.7 us -> 2.49 us  [shards(): pl.pallas_call(functools.partial(finish_kernel, 1.0 / math.sqrt(cells), 1...]
    unnamed x14 -> x0, local copies, waits for them, and re-layouts: 5.53 us -> none
    pallas_call x1, Pallas kernels: 44.6 us -> 43 us  [shards(): pl.pallas_call(functools.partial(main_kernel, n_wide, n_narrow), out_shap...]
where the time goes in v3:
time: 46.3 us; the launch traced here: 46.1 us
  Pallas kernels  45.5 us (98%)
  between operations  0.64 us (1%)
    pallas_call x1, Pallas kernels, shards(): pl.pallas_call(functools.partial(main_kernel, n_wide, n_narrow), out_shap...  43 us
    pallas_call x1, Pallas kernels, shards(): pl.pallas_call(functools.partial(finish_kernel, 1.0 / math.sqrt(cells), 1...  2.49 us

profile of v3, /device:TPU:1, one launch (start us, length us, event | category | flops | bytes accessed | tf_op | source)
XLA Modules:
  0.0 46.1 jit_solution(3482757595584441620)
XLA Ops:
  0.6 43.0 %levels.1 = (bf16[512,128]{1,0:T(8,128)(2,1)}, bf16[512,128]{1,0:T(8,128)(2,1)}, f32[192,128]{1,0:T(8,128)}) custom-call(bf16[512,128]{1,0:T(8,128)(2,1)} %bitcast.16, bf16[512,128]{1,0:T(8,128)(2,1)} %bitcast.17, bf16[432,48]{1,0:T(8,128)(2,1)} %bitcast.18, bf16[432,32]{1,0:T(8,128)(2,1)} %bitcast.19), custom_call_target="tpu_custom_call" | custom-call | tf_op jit(solution)/shard_map/levels/pallas_call | solution.py:421
  43.7 2.5 %finish.1 = (f32[432,48]{1,0:T(8,128)}, f32[432,32]{1,0:T(8,128)}, bf16[512,128]{1,0:T(8,128)(2,1)}, bf16[512,128]{1,0:T(8,128)(2,1)}) custom-call(f32[192,128]{1,0:T(8,128)} %get-tuple-element.11.turn, bf16[512,128]{1,0:T(8,128)(2,1)} %get-tuple-element.12.out_in, bf16[512,128]{1,0:T(8,128)(2,1)} %get-tuple-element.13.gf_in), custom_call_target="tpu_custom_call" | custom-call | tf_op jit(solution)/shard_map/finish/pallas_call | solution.py:444

commit v4 on v3

--- a/solution.py
+++ b/solution.py
@@ -170,10 +170,10 @@
     for k, field in enumerate((fine, cot)):
         west = (side_row >= 4 * k) & (side_row < 4 * k + 4) & (side_want == side_row - 4 * k - 4) & first
         east = (side_row >= 16 + 4 * k) & (side_row < 20 + 4 * k) & (side_want == side_row - 16 - 4 * k + 128) & last
-        spread_side = (west | east).astype(F32).astype(BF16)
+        both = jnp.concatenate([spread, (west | east).astype(F32).astype(BF16)], axis=0)
         for part in range(6):
             at = part * 128
-            got = dot(ext_ref[k, at:at + 128, :], spread) + dot(turned[at:at + 128, :], spread_side)
+            got = dot(jnp.concatenate([ext_ref[k, at:at + 128, :], turned[at:at + 128, :]], axis=1), both)
             if part == 0:
                 got = jnp.where(top, got, 0.0)
             if part == 5:
@@ -225,16 +225,14 @@
     def lanes(parts):
         return jnp.concatenate(parts, axis=1)
 
-    grad = jnp.zeros((128, 512), F32)
-    grad_up = jnp.zeros((128, 384), F32)
-    grad_c = jnp.zeros((144, 32), F32)
-    for r in range(2, 10, 2):
-        lhs = lanes([own_cot(r), own_cot(r + 1)])
-        grad += dot_nt(lhs, lanes([fine[(2 * q - 1) * 128:(2 * q + 3) * 128, :] for q in (r, r + 1)]))
-        grad_up += dot_nt(lhs, lanes([act[(q - 2) * 128:(q + 1) * 128, :] for q in (r, r + 1)]))
-        mine = [jnp.where(own[0:32], gpre[(q - 1) * 128 + 32:(q - 1) * 128 + 64, :].astype(F32), 0.0).astype(BF16)
-                for q in (r, r + 1)]
-        grad_c += dot_nt(lanes([pool[(q - 1) * 48:(q + 2) * 48, :] for q in (r, r + 1)]), lanes(mine))
+    rows = range(2, 10)
+    lhs = lanes([own_cot(r) for r in rows])
+    grad = dot_nt(lhs, lanes([fine[(2 * r - 1) * 128:(2 * r + 3) * 128, :] for r in rows]))
+    grad_up = dot_nt(lhs, lanes([act[(r - 2) * 128:(r + 1) * 128, :] for r in rows]))
+    grad_c = dot_nt(
+        lanes([pool[(r - 1) * 48:(r + 2) * 48, :] for r in rows]),
+        lanes([jnp.where(own[0:32], gpre[(r - 1) * 128 + 32:(r - 1) * 128 + 64, :].astype(F32), 0.0).astype(BF16)
+               for r in rows]))
     dys = ((0, 1, 1), (1, 1, 2))
     taps = [jnp.concatenate([grad_c[t * 16:t * 16 + 16], jnp.zeros((16, 96), F32)], axis=1) for t in range(9)]
     none = jnp.zeros((16, 128), F32)
@@ -253,7 +251,7 @@
         sums[block * 32:block * 32 + 32, :] = jnp.where(lane < 96, total, pltpu.roll(extra, 96, 1))
     count, depth = sums_ref.shape[0], sums_ref.shape[1]
     for j in range(count):
-        sums_ref[j] = sums[j * depth:(j + 1) * depth, :]
+        sums_ref[j] = sums[j * depth:(j + 1) * depth, :].astype(sums_ref.dtype)
 
 
 def level_outputs(out_ref, gf_ref, w_fwd, w_gp, fine, act, gpre, keep_gj, flat, turn):
@@ -324,13 +322,13 @@
     for read in reads[:2]:
         read.wait()
     pack_own(f_ref, c_ref, ext, wide32, go_left, go_right)
-    for read in reads[2:]:
-        read.wait()
-    prepare_weights(fw_ref, cw_ref, wide_w, stack, w_fwd, w_bwd, stack_c, w_pre, w_gp)
     pl.semaphore_wait(barrier, 8 + g1 + g2 - 2)
     halo = halo_copies(near, ext, left, right, go_left, go_right, halo_send, halo_recv)
     for j in (4, 5, 6, 7, 2, 3, 0, 1):
         halo[j].start()
+    for read in reads[2:]:
+        read.wait()
+    prepare_weights(fw_ref, cw_ref, wide_w, stack, w_fwd, w_bwd, stack_c, w_pre, w_gp)
     for copy in halo:
         copy.wait_recv()
     level_gradients(n_wide, n_narrow, me_y, me_x, ext, left, right, mine,
@@ -356,36 +354,45 @@
     for write in writes:
         write.start()
     one.wait_recv()
-    total = mine[me1]
+    total = mine[me1].astype(F32)
     for j in range(g1 - 1):
-        total += got1[j]
-    part[...] = total
+        total += got1[j].astype(F32)
+    part[...] = total.astype(part.dtype)
     send_all(second, lambda k: part, lambda j: got2.at[me2], send2, recv2)
-    got2[me2] = total
+    got2[me2] = part[...]
     for copy in halo:
         copy.wait_send()
     one.wait_send()
     for write in writes:
         write.wait()
     two.wait_recv()
-    total = got2[0]
+    total = got2[0].astype(F32)
     for k in range(1, g2):
-        total += got2[k]
-    fin[me1] = total
+        total += got2[k].astype(F32)
+    fin[me1] = total.astype(fin.dtype)
     send_all(first, lambda k: fin.at[me1], lambda j: fin.at[me1], send3, recv3)
     two.wait_send()
     three.wait_recv()
     for j in range(g1):
-        total_ref[j * depth:(j + 1) * depth, :] = fin[j]
+        total_ref[j * depth:(j + 1) * depth, :] = fin[j].astype(F32)
     three.wait_send()
 
 
-def finish_kernel(scale_fine, scale_coarse, turn, out_in, gf_in, gfine_ref, gcoarse_ref, out_ref, gf_ref, sem):
-    copies = [pltpu.make_async_copy(out_in, out_ref, sem.at[0]), pltpu.make_async_copy(gf_in, gf_ref, sem.at[1])]
-    for copy in copies:
-        copy.start()
+def finish_kernel(scale_fine, scale_coarse, turn_in, out_in, gf_in, gfine_out, gcoarse_out, out_ref, gf_ref,
+                  turn, out_v, gf_v, gfine_ref, gcoarse_ref, sem):
+    def copy(src, dst, j):
+        return pltpu.make_async_copy(src, dst, sem.at[j])
+
+    reads = [copy(turn_in, turn, 0), copy(out_in, out_v, 1), copy(gf_in, gf_v, 2)]
+    writes = [copy(out_v, out_ref, 3), copy(gf_v, gf_ref, 4)]
+    for read in reads:
+        read.start()
+    reads[0].wait()
     lane = iota((16, 128), 1)
     for ky in range(3):
+        if ky:
+            reads[ky].wait()
+            writes[ky - 1].start()
         flow = [turn[ky * 32 + z * 16:ky * 32 + z * 16 + 16, :] for z in range(2)]
         rise = [turn[96 + ky * 32 + z * 16:96 + ky * 32 + z * 16 + 16, :] for z in range(2)]
         ups = (rise[1], rise[0] + rise[1], rise[0])
@@ -404,8 +411,12 @@
                     gcoarse_ref[at:at + 16, :] = coarse
                 else:
                     gcoarse_ref[at:at + 16, :] = jnp.zeros((16, 32), F32)
-    for copy in copies:
-        copy.wait()
+        for j, (src, dst) in enumerate(((gfine_ref, gfine_out), (gcoarse_ref, gcoarse_out))):
+            rows = pl.ds(ky * 144, 144)
+            writes.append(copy(src.at[rows, :], dst.at[rows, :], 5 + 2 * ky + j))
+            writes[-1].start()
+    for write in writes:
+        write.wait()
 
 
 def shards(n_wide, n_narrow, features, cotangent, coarse_weight, fine_weight):
@@ -433,8 +444,8 @@
             VMEM((1280, 128), BF16), VMEM((1280, 128), BF16), VMEM((1024, 128), F32),
             VMEM((512, 256), BF16), VMEM((512, 128), F32), VMEM((ROWS, 128), F32),
             VMEM((512, 128), BF16), VMEM((512, 128), BF16), dma((2,)),
-            VMEM((g1, depth, 128), F32), VMEM((g1 - 1, depth, 128), F32), VMEM((depth, 128), F32),
-            VMEM((g2, depth, 128), F32), VMEM((g1, depth, 128), F32),
+            VMEM((g1, depth, 128), F32), VMEM((g1 - 1, depth, 128), F32), VMEM((depth, 128), BF16),
+            VMEM((g2, depth, 128), BF16), VMEM((g1, depth, 128), F32),
             dma, dma, dma, dma, dma, dma,
         ],
         compiler_params=pltpu.CompilerParams(
@@ -444,9 +455,10 @@
     gfine, gcoarse, output, grad_features = pl.pallas_call(
         functools.partial(finish_kernel, 1.0 / math.sqrt(cells), 1.0 / math.sqrt(cells // 8)),
         out_shape=(shape((432, 48), F32), shape((432, 32), F32), shape((512, 128), BF16), shape((512, 128), BF16)),
-        in_specs=[inside] * 3,
-        out_specs=(inside, inside, large, large),
-        scratch_shapes=[dma((2,))],
+        in_specs=[large] * 3,
+        out_specs=(large,) * 4,
+        scratch_shapes=[VMEM((ROWS, 128), F32), VMEM((512, 128), BF16), VMEM((512, 128), BF16),
+                        VMEM((432, 48), F32), VMEM((432, 32), F32), dma((11,))],
         name="finish",
     )(sums, output, grad_features)
     return (

time: 46.3 us -> 44 us (0.950)
  Pallas kernels: 45.5 us -> 43.2 us
    pallas_call x1, Pallas kernels: 43 us -> 41.2 us  [shards(): pl.pallas_call(functools.partial(main_kernel, n_wide, n_narrow), out_shap...]
    pallas_call x1, Pallas kernels: 2.49 us -> 1.99 us  [shards(): pl.pallas_call(functools.partial(finish_kernel, 1.0 / math.sqrt(cells), 1...]
where the time goes in v4:
time: 44 us; the launch traced here: 43.8 us
  Pallas kernels  43.2 us (98%)
  between operations  0.64 us (1%)
    pallas_call x1, Pallas kernels, shards(): pl.pallas_call(functools.partial(main_kernel, n_wide, n_narrow), out_shap...  41.2 us
    pallas_call x1, Pallas kernels, shards(): pl.pallas_call(functools.partial(finish_kernel, 1.0 / math.sqrt(cells), 1...  1.99 us

profile of v4, /device:TPU:1, one launch (start us, length us, event | category | flops | bytes accessed | tf_op | source)
XLA Modules:
  0.0 43.8 jit_solution(17217909134663578663)
XLA Ops:
  0.6 41.2 %levels.1 = (bf16[512,128]{1,0:T(8,128)(2,1)}, bf16[512,128]{1,0:T(8,128)(2,1)}, f32[192,128]{1,0:T(8,128)}) custom-call(bf16[512,128]{1,0:T(8,128)(2,1)} %bitcast.16, bf16[512,128]{1,0:T(8,128)(2,1)} %bitcast.17, bf16[432,48]{1,0:T(8,128)(2,1)} %bitcast.18, bf16[432,32]{1,0:T(8,128)(2,1)} %bitcast.19), custom_call_target="tpu_custom_call" | custom-call | tf_op jit(solution)/shard_map/levels/pallas_call | solution.py:432
  41.8 2.0 %finish.1 = (f32[432,48]{1,0:T(8,128)}, f32[432,32]{1,0:T(8,128)}, bf16[512,128]{1,0:T(8,128)(2,1)}, bf16[512,128]{1,0:T(8,128)(2,1)}) custom-call(f32[192,128]{1,0:T(8,128)} %get-tuple-element.11.turn_in, bf16[512,128]{1,0:T(8,128)(2,1)} %get-tuple-element.12.out_in, bf16[512,128]{1,0:T(8,128)(2,1)} %get-tuple-element.13.gf_in), custom_call_target="tpu_custom_call" | custom-call | tf_op jit(solution)/shard_map/finish/pallas_call | solution.py:455

commit v5 on v4

--- a/solution.py
+++ b/solution.py
@@ -13,6 +13,7 @@
 VMEM = pltpu.VMEM
 OUTER = 4
 ROWS = 192
+GRANT = 55040 * 1024
 
 
 def dot(a, b):
@@ -378,20 +379,19 @@
     three.wait_send()
 
 
-def finish_kernel(scale_fine, scale_coarse, turn_in, out_in, gf_in, gfine_out, gcoarse_out, out_ref, gf_ref,
-                  turn, out_v, gf_v, gfine_ref, gcoarse_ref, sem):
+def finish_kernel(scale_fine, scale_coarse, turn, out_in, gf_in, gfine_out, gcoarse_out, out_ref, gf_ref,
+                  out_v, gf_v, gfine_ref, gcoarse_ref, sem):
     def copy(src, dst, j):
         return pltpu.make_async_copy(src, dst, sem.at[j])
 
-    reads = [copy(turn_in, turn, 0), copy(out_in, out_v, 1), copy(gf_in, gf_v, 2)]
+    reads = [copy(out_in, out_v, 1), copy(gf_in, gf_v, 2)]
     writes = [copy(out_v, out_ref, 3), copy(gf_v, gf_ref, 4)]
     for read in reads:
         read.start()
-    reads[0].wait()
     lane = iota((16, 128), 1)
     for ky in range(3):
         if ky:
-            reads[ky].wait()
+            reads[ky - 1].wait()
             writes[ky - 1].start()
         flow = [turn[ky * 32 + z * 16:ky * 32 + z * 16 + 16, :] for z in range(2)]
         rise = [turn[96 + ky * 32 + z * 16:96 + ky * 32 + z * 16 + 16, :] for z in range(2)]
@@ -428,7 +428,7 @@
     fw = jnp.transpose(fine_weight, (2, 3, 4, 0, 1)).reshape(432, 48)
     cw = jnp.transpose(coarse_weight, (2, 3, 4, 1, 0)).reshape(432, 32)
     dma = pltpu.SemaphoreType.DMA
-    large = pl.BlockSpec(memory_space=pl.ANY)
+    large = pl.BlockSpec(memory_space=pltpu.HBM)
     output, grad_features, sums = pl.pallas_call(
         functools.partial(main_kernel, n_wide, n_narrow),
         out_shape=(shape((512, 128), BF16), shape((512, 128), BF16), shape((ROWS, 128), F32)),
@@ -449,16 +449,17 @@
             dma, dma, dma, dma, dma, dma,
         ],
         compiler_params=pltpu.CompilerParams(
-            collective_id=0, has_side_effects=True, vmem_limit_bytes=56 * 1024 * 1024),
+            collective_id=0, has_side_effects=True, vmem_limit_bytes=GRANT),
         name="levels",
     )(features.reshape(512, 128), cotangent.reshape(512, 128), fw, cw)
     gfine, gcoarse, output, grad_features = pl.pallas_call(
         functools.partial(finish_kernel, 1.0 / math.sqrt(cells), 1.0 / math.sqrt(cells // 8)),
         out_shape=(shape((432, 48), F32), shape((432, 32), F32), shape((512, 128), BF16), shape((512, 128), BF16)),
-        in_specs=[large] * 3,
+        in_specs=[inside, large, large],
         out_specs=(large,) * 4,
-        scratch_shapes=[VMEM((ROWS, 128), F32), VMEM((512, 128), BF16), VMEM((512, 128), BF16),
+        scratch_shapes=[VMEM((512, 128), BF16), VMEM((512, 128), BF16),
                         VMEM((432, 48), F32), VMEM((432, 32), F32), dma((11,))],
+        compiler_params=pltpu.CompilerParams(vmem_limit_bytes=GRANT),
         name="finish",
     )(sums, output, grad_features)
     return (

time: 44 us -> 43.2 us (0.982)
  Pallas kernels: 43.2 us -> 42.4 us
    pallas_call x1, Pallas kernels: 41.2 us -> 40.6 us  [shards(): pl.pallas_call(functools.partial(main_kernel, n_wide, n_narrow), out_shap...]
where the time goes in v5:
time: 43.2 us; the launch traced here: 43.1 us
  Pallas kernels  42.4 us (98%)
  between operations  0.64 us (1%)
    pallas_call x1, Pallas kernels, shards(): pl.pallas_call(functools.partial(main_kernel, n_wide, n_narrow), out_shap...  40.6 us
    pallas_call x1, Pallas kernels, shards(): pl.pallas_call(functools.partial(finish_kernel, 1.0 / math.sqrt(cells), 1...  1.89 us

profile of v5, /device:TPU:1, one launch (start us, length us, event | category | flops | bytes accessed | tf_op | source)
XLA Modules:
  0.0 43.1 jit_solution(18253655721569747661)
XLA Ops:
  0.6 40.6 %levels.1 = (bf16[512,128]{1,0:T(8,128)(2,1)}, bf16[512,128]{1,0:T(8,128)(2,1)}, f32[192,128]{1,0:T(8,128)S(1)}) custom-call(bf16[512,128]{1,0:T(8,128)(2,1)} %bitcast.16, bf16[512,128]{1,0:T(8,128)(2,1)} %bitcast.17, bf16[432,48]{1,0:T(8,128)(2,1)} %bitcast.18, bf16[432,32]{1,0:T(8,128)(2,1)} %bitcast.19), custom_call_target="tpu_custom_call" | custom-call | tf_op jit(solution)/shard_map/levels/pallas_call | solution.py:432
  41.2 1.9 %finish.1 = (f32[432,48]{1,0:T(8,128)}, f32[432,32]{1,0:T(8,128)}, bf16[512,128]{1,0:T(8,128)(2,1)}, bf16[512,128]{1,0:T(8,128)(2,1)}) custom-call(f32[192,128]{1,0:T(8,128)S(1)} %get-tuple-element.11.turn, bf16[512,128]{1,0:T(8,128)(2,1)} %get-tuple-element.12.out_in, bf16[512,128]{1,0:T(8,128)(2,1)} %get-tuple-element.13.gf_in), custom_call_target="tpu_custom_call" | custom-call | tf_op jit(solution)/shard_map/finish/pallas_call | solution.py:455

commit v6 on v5

--- a/solution.py
+++ b/solution.py
@@ -197,6 +197,16 @@
     inside = ((lane >= 2) | ((lane == 1) & first)) & ((lane <= 65) | ((lane == 66) & last))
     own = (iota((128, 128), 1) >= 2) & (iota((128, 128), 1) <= 65)
     blank = jnp.zeros((32, 128), BF16)
+
+    def own_cot(r):
+        a, b = 2 * r * 128, (2 * r + 1) * 128
+        both = jnp.concatenate([cot[a + 32:a + 96, :], cot[b + 32:b + 96, :]], axis=0)
+        return jnp.where(own, both.astype(F32), 0.0).astype(BF16)
+
+    def lanes(parts):
+        return jnp.concatenate(parts, axis=1)
+
+    grad = jnp.zeros((128, 512), F32)
     for r in range(1, 11):
         pre = dot(w_pre[...], pool[(r - 1) * 48:(r + 2) * 48, :])
         sig = 1.0 / (1.0 + jnp.exp(-pre))
@@ -217,18 +227,13 @@
             to[at + 96:at + 128, :] = blank
         if 2 <= r <= 9:
             keep_gj[(r - 2) * 128:(r - 1) * 128, :] = back[0:128]
-
-    def own_cot(r):
-        a, b = 2 * r * 128, (2 * r + 1) * 128
-        both = jnp.concatenate([cot[a + 32:a + 96, :], cot[b + 32:b + 96, :]], axis=0)
-        return jnp.where(own, both.astype(F32), 0.0).astype(BF16)
-
-    def lanes(parts):
-        return jnp.concatenate(parts, axis=1)
+        if r in (4, 8):
+            four = range(r - 2, r + 2)
+            grad += dot_nt(lanes([own_cot(q) for q in four]),
+                           lanes([fine[(2 * q - 1) * 128:(2 * q + 3) * 128, :] for q in four]))
 
     rows = range(2, 10)
     lhs = lanes([own_cot(r) for r in rows])
-    grad = dot_nt(lhs, lanes([fine[(2 * r - 1) * 128:(2 * r + 3) * 128, :] for r in rows]))
     grad_up = dot_nt(lhs, lanes([act[(r - 2) * 128:(r + 1) * 128, :] for r in rows]))
     grad_c = dot_nt(
         lanes([pool[(r - 1) * 48:(r + 2) * 48, :] for r in rows]),

time: 43.2 us -> 43.3 us (level)
  no operation moved by 1% of the time
where the time goes in v6:
time: 43.3 us; the launch traced here: 43.2 us
  Pallas kernels  42.5 us (98%)
  between operations  0.64 us (1%)
    pallas_call x1, Pallas kernels, shards(): pl.pallas_call(functools.partial(main_kernel, n_wide, n_narrow), out_shap...  40.6 us
    pallas_call x1, Pallas kernels, shards(): pl.pallas_call(functools.partial(finish_kernel, 1.0 / math.sqrt(cells), 1...  1.89 us

profile of v6, /device:TPU:1, one launch (start us, length us, event | category | flops | bytes accessed | tf_op | source)
XLA Modules:
  0.0 43.2 jit_solution(17291912709413491345)
XLA Ops:
  0.6 40.6 %levels.1 = (bf16[512,128]{1,0:T(8,128)(2,1)}, bf16[512,128]{1,0:T(8,128)(2,1)}, f32[192,128]{1,0:T(8,128)S(1)}) custom-call(bf16[512,128]{1,0:T(8,128)(2,1)} %bitcast.16, bf16[512,128]{1,0:T(8,128)(2,1)} %bitcast.17, bf16[432,48]{1,0:T(8,128)(2,1)} %bitcast.18, bf16[432,32]{1,0:T(8,128)(2,1)} %bitcast.19), custom_call_target="tpu_custom_call" | custom-call | tf_op jit(solution)/shard_map/levels/pallas_call | solution.py:437
  41.3 1.9 %finish.1 = (f32[432,48]{1,0:T(8,128)}, f32[432,32]{1,0:T(8,128)}, bf16[512,128]{1,0:T(8,128)(2,1)}, bf16[512,128]{1,0:T(8,128)(2,1)}) custom-call(f32[192,128]{1,0:T(8,128)S(1)} %get-tuple-element.11.turn, bf16[512,128]{1,0:T(8,128)(2,1)} %get-tuple-element.12.out_in, bf16[512,128]{1,0:T(8,128)(2,1)} %get-tuple-element.13.gf_in), custom_call_target="tpu_custom_call" | custom-call | tf_op jit(solution)/shard_map/finish/pallas_call | solution.py:460
